TPU v7x, 32 devices: a whole 2x2x4 slice. The times are simulated.
32 devices in a mesh: row: 4 (over x, core), col: 4 (over z), space: 2 (over y).
Axes of the slice: x: 2, y: 2, z: 4, core: 2. Of those that a mesh axis runs over, the one named last changes fastest.
Arguments:
- snapshots: bfloat16 [8192, 8192], P(('row', 'col'), 'space'), may hold values from -10 to 10
- ocean_mask: int32 [8192], P('space'), may hold values 0 or 1
- spread: float32 [], replicated, may hold values from 1 to 2
Outputs:
- affinity: float32 [3, 8192, 512], P(None, ('row', 'col'), 'space')
All inputs are finite; a program needn't handle non-finite values. No bound on the sum of `ocean_mask` on one device may be relied on, other than what follows from the above.
Results may differ from a plain program's by a relative error of at most 0.0003.
Values may be sent and summed in bfloat16 or wider, within the bound.
A program may use at most 64 MiB of HBM per device.

v0:
```python
import jax
import jax.numpy as jnp
from jax import lax
from jax.sharding import PartitionSpec as P

LAG = 240
BANDS = 3


def passed_along(block, axis, distance):
    devices = range(lax.axis_size(axis))
    route = [(i - distance, i) for i in devices if i - distance in devices]
    return lax.ppermute(block, axis, route)


def shifted(block, axis, distance):
    devices = range(lax.axis_size(axis))
    route = [((i - distance) % len(devices), i) for i in devices]
    return lax.ppermute(block, axis, route)


def combine_lags(earlier, later, extent):
    keep = earlier.shape[0] + later.shape[0] - extent - 1
    return earlier[-keep:, -keep:] + later[:keep, :keep]


def lag_sum(distance, window):
    extent = distance.shape[0]
    summed = None
    doubled = distance
    remaining = window
    while remaining:
        if remaining % 2 == 1:
            summed = doubled if summed is None else combine_lags(summed, doubled, extent)
        remaining = remaining // 2
        if remaining:
            doubled = combine_lags(doubled, doubled, extent)
    return summed


def square_norms(values):
    return jnp.sum(jnp.square(values.astype(jnp.float32)), axis=1)


def per_device(snapshots, ocean_mask, spread):
    block_rows = snapshots.shape[0]
    cells_dev = snapshots.shape[1]
    masked = snapshots * ocean_mask.astype(jnp.bfloat16)[None, :]
    history = passed_along(masked[block_rows - (LAG - 1) :], ("row", "col"), 1)
    own_rows = jnp.concatenate([history, masked], axis=0)
    partners = [own_rows]
    current = own_rows
    for offset in range(1, BANDS):
        current = shifted(current, "col", 1)
        partners.append(current)
    row_sq = square_norms(own_rows)
    lagged_list = []
    for partner in partners:
        col_sq = square_norms(partner)
        gram_tile = lax.dot_general(
            own_rows, partner, (((1,), (1,)), ((), ())), preferred_element_type=jnp.float32
        )
        distance = row_sq[:, None] + col_sq[None, :] - 2.0 * gram_tile
        lagged_list.append(lag_sum(distance, LAG))
    partial_dist = jnp.stack(lagged_list)
    column_width = block_rows // lax.axis_size("space")
    start_col = lax.axis_index("space") * column_width
    summed_dist = lax.psum(partial_dist, "space")
    lagged = lax.dynamic_slice_in_dim(summed_dist, start_col, column_width, 2)
    total_cells = cells_dev * lax.axis_size("space")
    kernel = jnp.exp(-lagged / (LAG * total_cells * spread))
    degree = lax.psum(jnp.sum(kernel, axis=(0, 2)), "space")
    degree_list = [degree]
    current_degree = degree
    for offset in range(1, BANDS):
        current_degree = shifted(current_degree, "col", 1)
        degree_list.append(current_degree)
    column_degrees = lax.dynamic_slice_in_dim(jnp.stack(degree_list), start_col, column_width, 1)
    factor = float(BANDS * block_rows)
    return factor * kernel / jnp.sqrt(degree[None, :, None] * column_degrees[:, None, :])


def solution(mesh):
    placed = (P(("row", "col"), "space"), P("space"), P())
    return jax.shard_map(
        per_device,
        mesh=mesh,
        in_specs=placed,
        out_specs=P(None, ("row", "col"), "space"),
        check_vma=False,
    )
```

profile of v0, /device:TPU:0, one launch (start us, length us, event | category | flops | bytes accessed | tf_op | source)
XLA Modules:
  0.0 469.5 jit_solution(8356598086163410592)
XLA Ops:
  6.5 0.0 all-reduce.2.cloned.1.call-start
  6.5 0.7 convert_element_type.13
  7.3 2.5 broadcast_multiply_fusion
  9.7 0.6 slice.244
  10.3 5.1 %collective-permute-start = (bf16[239,4096]{1,0:T(8,128)(2,1)S(1)}, bf16[239,4096]{1,0:T(8,128)(2,1)S(1)}, u32[]{:S(2)}, u32[]{:S(2)}) collective-permute-start(bf16[239,4096]{1,0:T(8,128)(2,1)S(1)} %slice.244), channel_id=1, source_target_pairs={{0,2},{2,4},{4,6},{6,8},{8,10},{10,12},{12,14},{14,16},{16,18},{18... | collective-permute-start | bytes 5873672 | tf_op jit(solution)/shard_map/ppermute | solution.py:13
  15.4 41.9 %collective-permute-done = bf16[239,4096]{1,0:T(8,128)(2,1)S(1)} collective-permute-done((bf16[239,4096]{1,0:T(8,128)(2,1)S(1)}, bf16[239,4096]{1,0:T(8,128)(2,1)S(1)}, u32[]{:S(2)}, u32[]{:S(2)}) %collective-permute-start) | collective-permute-done | bytes 1957920 | tf_op jit(solution)/shard_map/ppermute | solution.py:13
  57.3 3.8 pad_maximum_fusion
  61.1 2.5 collective-permute-start.1
  63.6 2.3 multiply_reduce_fusion.2
  65.9 5.0 %multiply_subtract_fusion.2 = f32[751,751]{1,0:T(8,128)S(1)} fusion(f32[751]{0:T(1024)S(1)} %multiply_reduce_fusion.2, bf16[512,4096]{1,0:T(8,128)(2,1)S(1)} %broadcast_multiply_fusion, bf16[239,4096]{1,0:T(8,128)(2,1)S(1)} %collective-permute-done), kind=kOutput, calls=%fused_computation.13 | convolution fusion | flops 4634293248 | bytes 8411200 | tf_op jit(solution)/shard_map/dot_general | solution.py:60
  70.9 0.9 slice_add_fusion.5
  71.8 0.8 slice_add_fusion.4
  72.6 0.8 slice_add_fusion.8
  73.5 124.6 %collective-permute-done.1 = bf16[751,4096]{1,0:T(8,128)(2,1)S(1)} collective-permute-done((bf16[751,4096]{1,0:T(8,128)(2,1)}, bf16[751,4096]{1,0:T(8,128)(2,1)S(1)}, u32[]{:S(2)}, u32[]{:S(2)}) %collective-permute-start.1) | collective-permute-done | bytes 6152224 | tf_op jit(solution)/shard_map/ppermute | solution.py:19
  198.1 1.3 collective-permute-start.2
  199.3 0.7 slice_add_fusion.11
  200.0 0.5 slice.257
  200.5 0.6 slice_add_fusion.14
  201.1 0.5 slice.258
  201.6 0.6 slice_add_fusion.17
  202.2 0.1 slice.261
  202.3 0.5 fusion.9
  202.8 1.3 fusion.5
  204.2 1.3 multiply_reduce_fusion.1
  205.4 5.0 %multiply_subtract_fusion.1 = f32[751,751]{1,0:T(8,128)S(1)} fusion(bf16[751,4096]{1,0:T(8,128)(2,1)S(1)} %collective-permute-done.1, f32[751]{0:T(1024)S(1)} %multiply_reduce_fusion.1, f32[751]{0:T(1024)S(1)} %multiply_reduce_fusion.2, bf16[512,4096]{1,0:T(8,128)(2,1)S(1)} %broadcast_multiply_fusion, bf16[239,4096]{1,0:T(8,128)(2,1)S(1)} %collective-permute-done), kind=kOutput, calls=%fused_computation.12 | convolution fusion | flops 4634293248 | bytes 14566396 | tf_op jit(solution)/shard_map/dot_general | solution.py:60
  210.4 0.9 slice_add_fusion.3
  211.3 0.8 slice_add_fusion.2
  212.2 0.8 slice_add_fusion.7
  213.0 0.7 slice_add_fusion.10
  213.7 0.7 slice.281
  214.4 0.6 slice_add_fusion.13
  215.0 0.5 slice.282
  215.5 0.6 slice_add_fusion.16
  216.1 0.1 slice.285
  216.2 2.2 fusion.10
  218.4 117.1 %collective-permute-done.2 = bf16[751,4096]{1,0:T(8,128)(2,1)} collective-permute-done((bf16[751,4096]{1,0:T(8,128)(2,1)S(1)}, bf16[751,4096]{1,0:T(8,128)(2,1)}, u32[]{:S(2)}, u32[]{:S(2)}) %collective-permute-start.2) | collective-permute-done | bytes 6152224 | tf_op jit(solution)/shard_map/ppermute | solution.py:19
  335.5 4.0 multiply_reduce_fusion
  339.5 7.9 %multiply_subtract_fusion = f32[751,751]{1,0:T(8,128)S(1)} fusion(bf16[751,4096]{1,0:T(8,128)(2,1)} %collective-permute-done.2, f32[751]{0:T(1024)S(1)} %multiply_reduce_fusion, f32[751]{0:T(1024)S(1)} %multiply_reduce_fusion.2, bf16[512,4096]{1,0:T(8,128)(2,1)S(1)} %broadcast_multiply_fusion, bf16[239,4096]{1,0:T(8,128)(2,1)S(1)} %collective-permute-done), kind=kOutput, calls=%fused_computation.11 | convolution fusion | flops 4634293248 | bytes 14566396 | tf_op jit(solution)/shard_map/dot_general | solution.py:60
  347.4 0.8 slice_add_fusion.1
  348.3 0.9 slice_add_fusion
  349.2 0.8 slice_add_fusion.6
  350.0 0.7 slice_add_fusion.9
  350.7 0.6 slice_add_fusion.12
  351.3 0.9 slice_add_fusion.15
  352.2 0.5 fusion.11
  352.7 0.1 slice.309
  352.8 0.5 slice.306
  353.3 0.0 copy-start.1
  353.3 0.5 slice.305
  353.8 0.9 copy-done
  354.7 0.5 copy-done.1
  355.2 0.7 fusion.1
  355.9 0.5 copy-done.2
  356.4 2.0 pad_maximum_fusion.1
  358.4 0.0 all-reduce.2.cloned.1.call-update
  359.1 82.6 %all-reduce.2.cloned.1.call-done = f32[3,512,512]{2,1,0:T(8,128)} async-done(((f32[3,512,512]{2,1,0:T(8,128)}), f32[3,512,512]{2,1,0:T(8,128)}) %all-reduce.2.cloned.1.call-update) | async-done | bytes 3145744 | tf_op jit(solution)/shard_map/psum | solution.py:68
  441.7 1.7 fusion.6
  443.4 4.9 %psum.15 = f32[512]{0:T(512)S(1)} all-reduce(f32[512]{0:T(512)S(1)} %fusion.6), channel_id=1, replica_groups=mesh['row'=4,'col'=4,'space'=2] {'space'}, use_global_device_ids=true, to_apply=%region_5.0 | all-reduce | flops 512 | bytes 4096 | tf_op jit(solution)/shard_map/psum | solution.py:72
  448.3 1.5 collective-permute-start.3
  449.8 3.9 collective-permute-done.3
  453.7 0.0 collective-permute-start.4
  453.7 5.4 %collective-permute-done.4 = f32[512]{0:T(512)S(1)} collective-permute-done((f32[512]{0:T(512)S(1)}, f32[512]{0:T(512)S(1)}, u32[]{:S(2)}, u32[]{:S(2)}) %collective-permute-start.4) | collective-permute-done | bytes 2080 | tf_op jit(solution)/shard_map/ppermute | solution.py:19
  459.1 0.1 fusion.8
  459.2 3.0 rsqrt_multiply_fusion
  (2 shorter events, 0.0 us)
Async XLA Ops:
  6.5 435.1 %all-reduce.2.cloned.1.call-start = ((), (), s32[]{:S(2)}) async-start(), calls=%async_computation | async-start | bytes 6291456 | tf_op jit(solution)/shard_map/psum | solution.py:68
  10.3 47.0 %collective-permute-start = (bf16[239,4096]{1,0:T(8,128)(2,1)S(1)}, bf16[239,4096]{1,0:T(8,128)(2,1)S(1)}, u32[]{:S(2)}, u32[]{:S(2)}) collective-permute-start(bf16[239,4096]{1,0:T(8,128)(2,1)S(1)} %slice.244), channel_id=1, source_target_pairs={{0,2},{2,4},{4,6},{6,8},{8,10},{10,12},{12,14},{14,16},{16,18},{18... | collective-permute-start | bytes 5873672 | tf_op jit(solution)/shard_map/ppermute | solution.py:13
  61.1 136.9 %collective-permute-start.1 = (bf16[751,4096]{1,0:T(8,128)(2,1)}, bf16[751,4096]{1,0:T(8,128)(2,1)S(1)}, u32[]{:S(2)}, u32[]{:S(2)}) collective-permute-start(bf16[751,4096]{1,0:T(8,128)(2,1)} %pad_maximum_fusion), channel_id=1, source_target_pairs={{6,0},{0,2},{2,4},{4,6},{7,1},{1,3},{3,5},{5,7},{14,8},{8,10},{10,... | collective-permute-start | bytes 18456584 | tf_op jit(solution)/shard_map/ppermute | solution.py:19
  198.1 137.4 %collective-permute-start.2 = (bf16[751,4096]{1,0:T(8,128)(2,1)S(1)}, bf16[751,4096]{1,0:T(8,128)(2,1)}, u32[]{:S(2)}, u32[]{:S(2)}) collective-permute-start(bf16[751,4096]{1,0:T(8,128)(2,1)S(1)} %collective-permute-done.1), channel_id=1, source_target_pairs={{6,0},{0,2},{2,4},{4,6},{7,1},{1,3},{3,5},{5,7},{14,8},{8,10},{10,... | collective-permute-start | bytes 18456584 | tf_op jit(solution)/shard_map/ppermute | solution.py:19
  353.3 1.4 copy-start
  353.3 1.9 copy-start.1
  355.2 1.2 copy-start.2
  448.3 5.4 %collective-permute-start.3 = (f32[512]{0:T(512)S(1)}, f32[512]{0:T(512)S(1)}, u32[]{:S(2)}, u32[]{:S(2)}) collective-permute-start(f32[512]{0:T(512)S(1)} %psum.15), channel_id=1, source_target_pairs={{6,0},{0,2},{2,4},{4,6},{7,1},{1,3},{3,5},{5,7},{14,8},{8,10},{10,... | collective-permute-start | bytes 6152 | tf_op jit(solution)/shard_map/ppermute | solution.py:19
  453.7 5.4 %collective-permute-start.4 = (f32[512]{0:T(512)S(1)}, f32[512]{0:T(512)S(1)}, u32[]{:S(2)}, u32[]{:S(2)}) collective-permute-start(f32[512]{0:T(512)S(1)} %collective-permute-done.3), channel_id=1, source_target_pairs={{6,0},{0,2},{2,4},{4,6},{7,1},{1,3},{3,5},{5,7},{14,8},{8,10},{10,... | collective-permute-start | bytes 6152 | tf_op jit(solution)/shard_map/ppermute | solution.py:19
Sparse Core Ops, SparseCore 0:
  358.6 83.0 all-reduce.1
where the time goes:
time: 478 us; the launch traced here: 469 us
  waiting for transfers between devices  375 us (78%)
  other arithmetic  37 us (8%)
  matrix products  17.9 us (4%)
  between operations  14.7 us (3%)
  starting transfers between devices  10.3 us (2%)
  local copies, waits for them, and re-layouts  9.14 us (2%)
  blocking collectives  4.94 us (1%)
    ppermute x4, waiting for transfers between devices, shifted(): return lax.ppermute(block, axis, route)  251 us
    psum x1, waiting for transfers between devices, per_device(): summed_dist = lax.psum(partial_dist, 'space')  82.6 us
    ppermute x1, waiting for transfers between devices, passed_along(): return lax.ppermute(block, axis, route)  41.9 us
    dot_general x3, matrix products, per_device(): lax.dot_general(own_rows, partner, (((1,), (1,)), ((), ())), preferred_el...  17.9 us
    add x18, other arithmetic, combine_lags(): return earlier[-keep:, -keep:] + later[:keep, :keep]  13.6 us
  transfers between devices with their start and end apart: 6, of which 6 were waited for; matrix products, arithmetic and copies ran while one was open for 6% of the time, Pallas kernels for 0%

commit v1 on v0

--- a/solution.py
+++ b/solution.py
@@ -79,11 +79,92 @@
     factor = float(BANDS * block_rows)
     return factor * kernel / jnp.sqrt(degree[None, :, None] * column_degrees[:, None, :])
 
+CHUNKS = 2
+
+
+def routed(block, axis, pairs):
+    return lax.ppermute(block, axis, pairs)
+
+
+def pick(condition, yes, no):
+    return lax.select(jnp.broadcast_to(condition, yes.shape), yes, no)
+
+
+def partial_lagged(rows, row_sq, columns, col_sq):
+    gram = lax.dot_general(rows, columns, (((1,), (1,)), ((), ())), preferred_element_type=jnp.float32)
+    distance = row_sq[:, None] + col_sq[None, :] - 2.0 * gram
+    return lag_sum(distance, LAG)[1:, 1:]
+
+
+def group_of_four(snapshots, ocean_mask, spread):
+    block_rows, cells_dev = snapshots.shape
+    spaces = lax.axis_size("space")
+    width = block_rows // spaces
+    slot = lax.axis_index("col")
+    here = lax.axis_index("space")
+    groups = lax.axis_size("row")
+    masked = snapshots * ocean_mask.astype(jnp.bfloat16)[None, :]
+    tail = masked[block_rows - LAG :]
+    step = block_rows // CHUNKS
+    chunks = [masked[i * step : (i + 1) * step] for i in range(CHUNKS)]
+
+    start_2 = routed(tail, ("row", "col"), [(4 * (g - 1) + 3, 4 * g + 2) for g in range(1, groups)])
+    tail2_1 = routed(tail, "col", [(2, 1)])
+    before, third, third_on, first_on = [], [], [], []
+    for chunk in chunks:
+        got = routed(chunk, "col", [(0, 1), (1, 2), (2, 3)])
+        far = routed(chunk, "col", [(3, 1)])
+        before.append(got)
+        third.append(far)
+        third_on.append(routed(far, "col", [(1, 0)]))
+        first_on.append(routed(got, "col", [(1, 2)]))
+    start_1 = routed(start_2, "col", [(2, 1)])
+    start_0 = routed(start_1, "col", [(1, 0)])
+    start = start_0 + start_1 + start_2
+    tail2_0 = routed(tail2_1, "col", [(1, 0)])
+    before = jnp.concatenate(before)
+    tail1_3 = routed(before[block_rows - LAG :], "col", [(2, 3)])
+    third = jnp.concatenate(third)
+    third_on = jnp.concatenate(third_on)
+    first_on = jnp.concatenate(first_on)
+
+    rows = jnp.concatenate([pick(slot == 0, start, before[block_rows - LAG :]), masked])
+    next_tail = pick(
+        slot == 1, start, pick(slot == 2, first_on[block_rows - LAG :], tail2_0 + tail1_3)
+    )
+    next_rows = jnp.concatenate([next_tail, before + third_on])
+    last_rows = jnp.concatenate([pick(slot == 1, tail2_1, start), pick(slot == 1, third, first_on)])
+
+    over = [(i, 1 - i) for i in range(2)]
+
+    def halves(tile, dim):
+        mine = lax.dynamic_slice_in_dim(tile, here * width, width, dim)
+        other = lax.dynamic_slice_in_dim(tile, (1 - here) * width, width, dim)
+        return mine + routed(other, "space", over)
+
+    row_sq = square_norms(rows)
+    lagged_0 = halves(partial_lagged(rows, row_sq, rows, row_sq), 1)
+    lagged_1 = halves(partial_lagged(rows, row_sq, next_rows, square_norms(next_rows)), 1)
+    tile_2 = partial_lagged(rows, row_sq, last_rows, square_norms(last_rows))
+    turned = routed(halves(tile_2, 0), "col", [(1, 3), (2, 0)]).T
+    inner = (slot == 1) | (slot == 2)
+    lagged_2 = pick(inner, halves(tile_2, 1), turned)
+    lagged = jnp.stack([lagged_0, lagged_1, lagged_2])
+
+    kernel = jnp.exp(-lagged / (LAG * cells_dev * spaces * spread))
+    half_degree = jnp.sum(kernel, axis=(0, 2))
+    degree = half_degree + routed(half_degree, "space", over)
+    degrees = [degree] + [shifted(degree, "col", offset) for offset in range(1, BANDS)]
+    column_degrees = lax.dynamic_slice_in_dim(jnp.stack(degrees), here * width, width, 1)
+    factor = float(BANDS * block_rows)
+    return factor * kernel / jnp.sqrt(degree[None, :, None] * column_degrees[:, None, :])
+
 
 def solution(mesh):
     placed = (P(("row", "col"), "space"), P("space"), P())
+    four = mesh.shape["col"] == 4 and mesh.shape["space"] == 2
     return jax.shard_map(
-        per_device,
+        group_of_four if four else per_device,
         mesh=mesh,
         in_specs=placed,
         out_specs=P(None, ("row", "col"), "space"),

time: 478 us -> 404 us (0.85)
  the two profiles are of different devices: /device:TPU:0 before, /device:TPU:2 now
where the time goes in v1:
time: 404 us; the launch traced here: 399 us
  waiting for transfers between devices  273 us (68%)
  other arithmetic  48.4 us (12%)
  starting transfers between devices  35.9 us (9%)
  matrix products  20.2 us (5%)
  local copies, waits for them, and re-layouts  20 us (5%)
    ppermute x20, waiting for transfers between devices, routed(): return lax.ppermute(block, axis, pairs)  268 us
    ppermute x20, starting transfers between devices, routed(): return lax.ppermute(block, axis, pairs)  35.9 us
    dot_general x3, matrix products, partial_lagged(): lax.dot_general(rows, columns, (((1,), (1,)), ((), ())), preferred_elemen...  20.2 us
    add x21, other arithmetic, combine_lags(): return earlier[-keep:, -keep:] + later[:keep, :keep]  19.5 us
    select_n x3, other arithmetic, pick(): return lax.select(jnp.broadcast_to(condition, yes.shape), yes, no)  11.2 us
  transfers between devices with their start and end apart: 22, of which 12 were waited for; matrix products, arithmetic and copies ran while one was open for 5% of the time, Pallas kernels for 0%

profile of v1, /device:TPU:2, one launch (start us, length us, event | category | flops | bytes accessed | tf_op | source)
XLA Modules:
  0.0 398.8 jit_solution(4250255497028358758)
XLA Ops:
  0.7 2.5 broadcast_multiply_fusion
  6.7 1.9 collective-permute-start.6
  8.7 4.0 collective-permute-start.3
  12.7 7.0 %collective-permute-start.9 = (bf16[256,4096]{1,0:T(8,128)(2,1)S(1)}, bf16[256,4096]{1,0:T(8,128)(2,1)}, u32[]{:S(2)}, u32[]{:S(2)}) collective-permute-start(bf16[256,4096]{1,0:T(8,128)(2,1)S(1)} %get-tuple-element.7), channel_id=1, source_target_pairs={{0,2},{2,4},{4,6},{1,3},{3,5},{5,7},{8,10},{10,12},{12,14},{9,11},... | collective-permute-start | bytes 6291464 | tf_op jit(solution)/shard_map/ppermute | solution.py:86
  19.7 1.3 collective-permute-start.11
  21.0 1.3 collective-permute-start.13
  22.3 2.0 collective-permute-start.1
  24.3 34.2 %collective-permute-done.3 = bf16[256,4096]{1,0:T(8,128)(2,1)S(1)} collective-permute-done((bf16[256,4096]{1,0:T(8,128)(2,1)S(1)}, bf16[256,4096]{1,0:T(8,128)(2,1)S(1)}, u32[]{:S(2)}, u32[]{:S(2)}) %collective-permute-start.3) | collective-permute-done | bytes 2097184 | tf_op jit(solution)/shard_map/ppermute | solution.py:86
  58.5 2.0 collective-permute-start.5
  60.6 41.8 %collective-permute-done.9 = bf16[256,4096]{1,0:T(8,128)(2,1)} collective-permute-done((bf16[256,4096]{1,0:T(8,128)(2,1)S(1)}, bf16[256,4096]{1,0:T(8,128)(2,1)}, u32[]{:S(2)}, u32[]{:S(2)}) %collective-permute-start.9) | collective-permute-done | bytes 2097184 | tf_op jit(solution)/shard_map/ppermute | solution.py:86
  102.3 2.0 collective-permute-start.15
  104.3 1.4 slice.275
  105.7 1.3 collective-permute-start.7
  107.0 33.4 %collective-permute-done.11 = bf16[256,4096]{1,0:T(8,128)(2,1)S(1)} collective-permute-done((bf16[256,4096]{1,0:T(8,128)(2,1)S(1)}, bf16[256,4096]{1,0:T(8,128)(2,1)S(1)}, u32[]{:S(2)}, u32[]{:S(2)}) %collective-permute-start.11) | collective-permute-done | bytes 2097184 | tf_op jit(solution)/shard_map/ppermute | solution.py:86
  140.4 1.9 collective-permute-start.8
  142.3 24.9 %collective-permute-done.13 = bf16[256,4096]{1,0:T(8,128)(2,1)S(1)} collective-permute-done((bf16[256,4096]{1,0:T(8,128)(2,1)S(1)}, bf16[256,4096]{1,0:T(8,128)(2,1)S(1)}, u32[]{:S(2)}, u32[]{:S(2)}) %collective-permute-start.13) | collective-permute-done | bytes 2097184 | tf_op jit(solution)/shard_map/ppermute | solution.py:86
  167.2 1.3 collective-permute-start.2
  169.3 3.8 maximum_add_fusion
  173.3 3.6 maximum_select_fusion
  177.0 59.5 %collective-permute-done.7 = bf16[240,4096]{1,0:T(8,128)(2,1)} collective-permute-done((bf16[240,4096]{1,0:T(8,128)(2,1)}, bf16[240,4096]{1,0:T(8,128)(2,1)}, u32[]{:S(2)}, u32[]{:S(2)}) %collective-permute-start.7) | collective-permute-done | bytes 1966112 | tf_op jit(solution)/shard_map/ppermute | solution.py:86
  236.5 40.0 %collective-permute-done.2 = bf16[240,4096]{1,0:T(8,128)(2,1)} collective-permute-done((bf16[240,4096]{1,0:T(8,128)(2,1)}, bf16[240,4096]{1,0:T(8,128)(2,1)}, u32[]{:S(2)}, u32[]{:S(2)}) %collective-permute-start.2) | collective-permute-done | bytes 1966112 | tf_op jit(solution)/shard_map/ppermute | solution.py:86
  276.5 5.9 %fusion.2 = (bf16[240,4096]{1,0:T(8,128)(2,1)}, bf16[240,4096]{1,0:T(8,128)(2,1)S(1)}) fusion(bf16[256,4096]{1,0:T(8,128)(2,1)} %collective-permute-done.5, bf16[240,4096]{1,0:T(8,128)(2,1)} %collective-permute-done.7, bf16[240,4096]{1,0:T(8,128)(2,1)} %collective-permute-done.8, pred[]{:T(512)S(6)} %eq.15, pred[]{:T(512)S(6)} %eq.14, ...), kind=kLoop, calls=%fused_computation.33 | loop fusion | flops 4915200 | bytes 15728642 | tf_op jit(solution)/shard_map/select_n | solution.py:90
  282.4 1.7 broadcast_select_fusion.1
  284.0 1.9 copy-done.1
  285.9 1.3 multiply_reduce_fusion.2
  287.2 1.7 broadcast_add_fusion
  289.6 1.3 multiply_reduce_fusion.1
  291.1 5.0 %multiply_subtract_fusion.1 = f32[752,752]{1,0:T(8,128)S(1)} fusion(bf16[512,4096]{1,0:T(8,128)(2,1)S(1)} %maximum_add_fusion, bf16[240,4096]{1,0:T(8,128)(2,1)S(1)} %copy-done.5, f32[752]{0:T(1024)S(1)} %multiply_reduce_fusion.1, f32[752]{0:T(1024)S(1)} %multiply_reduce_fusion.2, bf16[512,4096]{1,0:T(8,128)(2,1)S(1)} %copy-done.1, ...), kind=kOutput, calls=%fused_computation.20 | convolution fusion | flops 4658946048 | bytes 14588800 | tf_op jit(solution)/shard_map/dot_general | solution.py:94
  296.1 0.9 slice_add_fusion.5
  297.0 0.8 slice_add_fusion.4
  297.8 0.8 slice_add_fusion.3
  300.0 1.0 slice_add_fusion.16
  301.0 1.5 slice.325
  302.5 1.5 slice.324
  304.0 1.3 multiply_reduce_fusion
  305.3 5.0 %multiply_subtract_fusion = f32[752,752]{1,0:T(8,128)S(1)} fusion(bf16[512,4096]{1,0:T(8,128)(2,1)S(1)} %maximum_select_fusion, bf16[240,4096]{1,0:T(8,128)(2,1)S(1)} %copy-done.4, f32[752]{0:T(1024)S(1)} %multiply_reduce_fusion, f32[752]{0:T(1024)S(1)} %multiply_reduce_fusion.2, bf16[512,4096]{1,0:T(8,128)(2,1)S(1)} %copy-done.1, ...), kind=kOutput, calls=%fused_computation.19 | convolution fusion | flops 4658946048 | bytes 14588800 | tf_op jit(solution)/shard_map/dot_general | solution.py:94
  310.2 0.9 slice_add_fusion.2
  311.1 0.8 slice_add_fusion.1
  312.0 0.8 slice_add_fusion
  316.1 2.0 fusion.5
  318.1 0.9 constant_dynamic-slice_fusion
  319.0 0.9 constant_dynamic-slice_fusion.1
  319.8 3.1 copy.5
  322.9 10.2 %multiply_subtract_fusion.2 = f32[752,752]{0,1:T(8,128)S(1)} fusion(f32[752,752]{0,1:T(8,128)} %copy.5, bf16[512,4096]{1,0:T(8,128)(2,1)} %copy-done, bf16[240,4096]{1,0:T(8,128)(2,1)} %copy-done.2), kind=kOutput, calls=%fused_computation.21 | convolution fusion | flops 4646060032 | bytes 10684416 | tf_op jit(solution)/shard_map/dot_general | solution.py:94
  333.1 0.8 slice_add_fusion.8
  334.0 0.8 slice_add_fusion.7
  339.2 1.5 collective-permute-start.17
  340.7 1.9 fusion.6
  343.4 1.1 collective-permute-start.14
  344.6 1.2 collective-permute-start.16
  345.7 1.8 fusion.7
  349.3 4.8 %collective-permute-done.17 = f32[256,512]{1,0:T(8,128)S(1)} collective-permute-done((f32[256,512]{1,0:T(8,128)S(1)}, f32[256,512]{1,0:T(8,128)S(1)}, u32[]{:S(2)}, u32[]{:S(2)}) %collective-permute-start.17) | collective-permute-done | bytes 524320 | tf_op jit(solution)/shard_map/ppermute | solution.py:86
  354.0 0.9 dynamic-slice_add_fusion
  354.9 1.3 collective-permute-start.18
  356.2 9.1 %collective-permute-done.14 = f32[512,256]{1,0:T(8,128)S(1)} collective-permute-done((f32[512,256]{1,0:T(8,128)S(1)}, f32[512,256]{1,0:T(8,128)S(1)}, u32[]{:S(2)}, u32[]{:S(2)}) %collective-permute-start.14) | collective-permute-done | bytes 524320 | tf_op jit(solution)/shard_map/ppermute | solution.py:86
  365.6 11.0 %collective-permute-done.16 = f32[512,256]{1,0:T(8,128)} collective-permute-done((f32[512,256]{1,0:T(8,128)}, f32[512,256]{1,0:T(8,128)}, u32[]{:S(2)}, u32[]{:S(2)}) %collective-permute-start.16) | collective-permute-done | bytes 524320 | tf_op jit(solution)/shard_map/ppermute | solution.py:86
  376.6 1.1 dynamic-slice_add_fusion.1
  378.0 6.8 %collective-permute-done.4 = f32[512,256]{0,1:T(8,128)} collective-permute-done((f32[512,256]{0,1:T(8,128)}, f32[512,256]{0,1:T(8,128)}, u32[]{:S(2)}, u32[]{:S(2)}) %collective-permute-start.4) | collective-permute-done | bytes 524320 | tf_op jit(solution)/shard_map/ppermute | solution.py:86
  384.8 1.1 add_bitcast_fusion.1
  385.9 1.1 fusion.8
  387.4 1.6 collective-permute-start.19
  388.9 2.1 collective-permute-done.19
  391.0 5.4 %collective-permute-done.20 = f32[512]{0:T(512)S(1)} collective-permute-done((f32[512]{0:T(512)S(1)}, f32[512]{0:T(512)S(1)}, u32[]{:S(2)}, u32[]{:S(2)}) %collective-permute-start.20) | collective-permute-done | bytes 2080 | tf_op jit(solution)/shard_map/ppermute | solution.py:19
  396.9 1.6 copy.10
  (77 shorter events, 18.2 us)
Async XLA Ops:
  3.2 2.0 copy-start
  3.4 9.3 %collective-permute-start = (bf16[240,4096]{1,0:T(8,128)(2,1)S(1)}, bf16[240,4096]{1,0:T(8,128)(2,1)S(1)}, u32[]{:S(2)}, u32[]{:S(2)}) collective-permute-start(bf16[240,4096]{1,0:T(8,128)(2,1)S(1)} %slice.273), channel_id=1, source_target_pairs={{6,12},{14,20},{22,28},{7,13},{15,21},{23,29}} | collective-permute-start | bytes 5898248 | tf_op jit(solution)/shard_map/ppermute | solution.py:86
  5.1 14.6 %collective-permute-start.10 = (bf16[256,4096]{1,0:T(8,128)(2,1)S(1)}, bf16[256,4096]{1,0:T(8,128)(2,1)S(1)}, u32[]{:S(2)}, u32[]{:S(2)}) collective-permute-start(bf16[256,4096]{1,0:T(8,128)(2,1)S(1)} %get-tuple-element.7), channel_id=1, source_target_pairs={{6,2},{7,3},{14,10},{15,11},{22,18},{23,19},{30,26},{31,27}} | collective-permute-start | bytes 6291464 | tf_op jit(solution)/shard_map/ppermute | solution.py:86
  5.9 15.1 %collective-permute-start.12 = (bf16[256,4096]{1,0:T(8,128)(2,1)S(1)}, bf16[256,4096]{1,0:T(8,128)(2,1)S(1)}, u32[]{:S(2)}, u32[]{:S(2)}) collective-permute-start(bf16[256,4096]{1,0:T(8,128)(2,1)S(1)} %get-tuple-element.8), channel_id=1, source_target_pairs={{6,2},{7,3},{14,10},{15,11},{22,18},{23,19},{30,26},{31,27}} | collective-permute-start | bytes 6291464 | tf_op jit(solution)/shard_map/ppermute | solution.py:86
  6.7 15.6 %collective-permute-start.6 = (bf16[240,4096]{1,0:T(8,128)(2,1)S(1)}, bf16[240,4096]{1,0:T(8,128)(2,1)}, u32[]{:S(2)}, u32[]{:S(2)}) collective-permute-start(bf16[240,4096]{1,0:T(8,128)(2,1)S(1)} %slice.273), channel_id=1, source_target_pairs={{4,2},{5,3},{12,10},{13,11},{20,18},{21,19},{28,26},{29,27}} | collective-permute-start | bytes 5898248 | tf_op jit(solution)/shard_map/ppermute | solution.py:86
  8.7 49.9 %collective-permute-start.3 = (bf16[256,4096]{1,0:T(8,128)(2,1)S(1)}, bf16[256,4096]{1,0:T(8,128)(2,1)S(1)}, u32[]{:S(2)}, u32[]{:S(2)}) collective-permute-start(bf16[256,4096]{1,0:T(8,128)(2,1)S(1)} %get-tuple-element.8), channel_id=1, source_target_pairs={{0,2},{2,4},{4,6},{1,3},{3,5},{5,7},{8,10},{10,12},{12,14},{9,11},... | collective-permute-start | bytes 6291464 | tf_op jit(solution)/shard_map/ppermute | solution.py:86
  12.7 155.9 %copy-start.14 = (bf16[240,4096]{1,0:T(8,128)(2,1)}, bf16[240,4096]{1,0:T(8,128)(2,1)S(1)}, u32[]{:S(2)}) copy-start(bf16[240,4096]{1,0:T(8,128)(2,1)S(1)} %collective-permute-done) | copy-start | bytes 5898244
  12.7 89.7 %collective-permute-start.9 = (bf16[256,4096]{1,0:T(8,128)(2,1)S(1)}, bf16[256,4096]{1,0:T(8,128)(2,1)}, u32[]{:S(2)}, u32[]{:S(2)}) collective-permute-start(bf16[256,4096]{1,0:T(8,128)(2,1)S(1)} %get-tuple-element.7), channel_id=1, source_target_pairs={{0,2},{2,4},{4,6},{1,3},{3,5},{5,7},{8,10},{10,12},{12,14},{9,11},... | collective-permute-start | bytes 6291464 | tf_op jit(solution)/shard_map/ppermute | solution.py:86
  19.7 38.8 %copy-start.8 = (bf16[256,4096]{1,0:T(8,128)(2,1)}, bf16[256,4096]{1,0:T(8,128)(2,1)S(1)}, u32[]{:S(2)}) copy-start(bf16[256,4096]{1,0:T(8,128)(2,1)S(1)} %collective-permute-done.10) | copy-start | bytes 6291460
  19.7 120.7 %collective-permute-start.11 = (bf16[256,4096]{1,0:T(8,128)(2,1)S(1)}, bf16[256,4096]{1,0:T(8,128)(2,1)S(1)}, u32[]{:S(2)}, u32[]{:S(2)}) collective-permute-start(bf16[256,4096]{1,0:T(8,128)(2,1)S(1)} %collective-permute-done.10), channel_id=1, source_target_pairs={{2,0},{3,1},{10,8},{11,9},{18,16},{19,17},{26,24},{27,25}} | collective-permute-start | bytes 6291464 | tf_op jit(solution)/shard_map/ppermute | solution.py:86
  21.0 119.4 %copy-start.10 = (bf16[256,4096]{1,0:T(8,128)(2,1)}, bf16[256,4096]{1,0:T(8,128)(2,1)S(1)}, u32[]{:S(2)}) copy-start(bf16[256,4096]{1,0:T(8,128)(2,1)S(1)} %collective-permute-done.12) | copy-start | bytes 6291460
  21.0 146.2 %collective-permute-start.13 = (bf16[256,4096]{1,0:T(8,128)(2,1)S(1)}, bf16[256,4096]{1,0:T(8,128)(2,1)S(1)}, u32[]{:S(2)}, u32[]{:S(2)}) collective-permute-start(bf16[256,4096]{1,0:T(8,128)(2,1)S(1)} %collective-permute-done.12), channel_id=1, source_target_pairs={{2,0},{3,1},{10,8},{11,9},{18,16},{19,17},{26,24},{27,25}} | collective-permute-start | bytes 6291464 | tf_op jit(solution)/shard_map/ppermute | solution.py:86
  22.3 83.4 %collective-permute-start.1 = (bf16[240,4096]{1,0:T(8,128)(2,1)S(1)}, bf16[240,4096]{1,0:T(8,128)(2,1)}, u32[]{:S(2)}, u32[]{:S(2)}) collective-permute-start(bf16[240,4096]{1,0:T(8,128)(2,1)S(1)} %collective-permute-done), channel_id=1, source_target_pairs={{4,2},{5,3},{12,10},{13,11},{20,18},{21,19},{28,26},{29,27}} | collective-permute-start | bytes 5898248 | tf_op jit(solution)/shard_map/ppermute | solution.py:86
  58.5 114.6 %collective-permute-start.5 = (bf16[256,4096]{1,0:T(8,128)(2,1)S(1)}, bf16[256,4096]{1,0:T(8,128)(2,1)}, u32[]{:S(2)}, u32[]{:S(2)}) collective-permute-start(bf16[256,4096]{1,0:T(8,128)(2,1)S(1)} %collective-permute-done.3), channel_id=1, source_target_pairs={{2,4},{3,5},{10,12},{11,13},{18,20},{19,21},{26,28},{27,29}} | collective-permute-start | bytes 6291464 | tf_op jit(solution)/shard_map/ppermute | solution.py:86
  102.3 70.8 %collective-permute-start.15 = (bf16[256,4096]{1,0:T(8,128)(2,1)}, bf16[256,4096]{1,0:T(8,128)(2,1)}, u32[]{:S(2)}, u32[]{:S(2)}) collective-permute-start(bf16[256,4096]{1,0:T(8,128)(2,1)} %collective-permute-done.9), channel_id=1, source_target_pairs={{2,4},{3,5},{10,12},{11,13},{18,20},{19,21},{26,28},{27,29}} | collective-permute-start | bytes 6291464 | tf_op jit(solution)/shard_map/ppermute | solution.py:86
  105.7 130.7 %collective-permute-start.7 = (bf16[240,4096]{1,0:T(8,128)(2,1)}, bf16[240,4096]{1,0:T(8,128)(2,1)}, u32[]{:S(2)}, u32[]{:S(2)}) collective-permute-start(bf16[240,4096]{1,0:T(8,128)(2,1)} %collective-permute-done.6), channel_id=1, source_target_pairs={{2,0},{3,1},{10,8},{11,9},{18,16},{19,17},{26,24},{27,25}} | collective-permute-start | bytes 5898248 | tf_op jit(solution)/shard_map/ppermute | solution.py:86
  140.4 26.8 %copy-start.12 = (bf16[256,4096]{1,0:T(8,128)(2,1)}, bf16[256,4096]{1,0:T(8,128)(2,1)S(1)}, u32[]{:S(2)}) copy-start(bf16[256,4096]{1,0:T(8,128)(2,1)S(1)} %collective-permute-done.11) | copy-start | bytes 6291460
  140.4 96.1 %collective-permute-start.8 = (bf16[240,4096]{1,0:T(8,128)(2,1)}, bf16[240,4096]{1,0:T(8,128)(2,1)}, u32[]{:S(2)}, u32[]{:S(2)}) collective-permute-start(bf16[240,4096]{1,0:T(8,128)(2,1)} %slice.275), channel_id=1, source_target_pairs={{4,6},{5,7},{12,14},{13,15},{20,22},{21,23},{28,30},{29,31}} | collective-permute-start | bytes 5898248 | tf_op jit(solution)/shard_map/ppermute | solution.py:86
  167.2 1.4 copy-start.13
  167.2 109.2 %collective-permute-start.2 = (bf16[240,4096]{1,0:T(8,128)(2,1)}, bf16[240,4096]{1,0:T(8,128)(2,1)}, u32[]{:S(2)}, u32[]{:S(2)}) collective-permute-start(bf16[240,4096]{1,0:T(8,128)(2,1)} %collective-permute-done.1), channel_id=1, source_target_pairs={{2,0},{3,1},{10,8},{11,9},{18,16},{19,17},{26,24},{27,25}} | collective-permute-start | bytes 5898248 | tf_op jit(solution)/shard_map/ppermute | solution.py:86
  169.2 3.9 copy-start.9
  169.2 4.1 %copy-start.11 = (bf16[256,4096]{1,0:T(8,128)(2,1)S(1)}, bf16[256,4096]{1,0:T(8,128)(2,1)}, u32[]{:S(2)}) copy-start(bf16[256,4096]{1,0:T(8,128)(2,1)} %copy-done.10) | copy-start | bytes 6291460
  173.1 103.4 %copy-start.15 = (bf16[240,4096]{1,0:T(8,128)(2,1)S(1)}, bf16[240,4096]{1,0:T(8,128)(2,1)}, u32[]{:S(2)}) copy-start(bf16[240,4096]{1,0:T(8,128)(2,1)} %copy-done.14) | copy-start | bytes 5898244
  282.3 3.6 copy-start.1
  284.0 3.2 copy-start.2
  287.2 2.4 copy-start.5
  289.6 1.5 copy-start.3
  301.0 3.0 copy-start.4
  338.1 1.0 copy-start.16
  338.2 2.6 copy-start.6
  338.2 2.5 copy-start.7
  339.2 14.9 %collective-permute-start.17 = (f32[256,512]{1,0:T(8,128)S(1)}, f32[256,512]{1,0:T(8,128)S(1)}, u32[]{:S(2)}, u32[]{:S(2)}) collective-permute-start(f32[256,512]{1,0:T(8,128)S(1)} %copy-done.16), channel_id=1, source_target_pairs={{0,1},{1,0},{2,3},{3,2},{4,5},{5,4},{6,7},{7,6},{8,9},{9,8},{10,11... | collective-permute-start | bytes 1572872 | tf_op jit(solution)/shard_map/ppermute | solution.py:86
  343.4 21.8 %collective-permute-start.14 = (f32[512,256]{1,0:T(8,128)S(1)}, f32[512,256]{1,0:T(8,128)S(1)}, u32[]{:S(2)}, u32[]{:S(2)}) collective-permute-start(f32[512,256]{1,0:T(8,128)S(1)} %constant_dynamic-slice_fusion.2), channel_id=1, source_target_pairs={{0,1},{1,0},{2,3},{3,2},{4,5},{5,4},{6,7},{7,6},{8,9},{9,8},{10,11... | collective-permute-start | bytes 1572872 | tf_op jit(solution)/shard_map/ppermute | solution.py:86
  344.6 32.1 %collective-permute-start.16 = (f32[512,256]{1,0:T(8,128)}, f32[512,256]{1,0:T(8,128)}, u32[]{:S(2)}, u32[]{:S(2)}) collective-permute-start(f32[512,256]{1,0:T(8,128)} %constant_dynamic-slice_fusion.1), channel_id=1, source_target_pairs={{0,1},{1,0},{2,3},{3,2},{4,5},{5,4},{6,7},{7,6},{8,9},{9,8},{10,11... | collective-permute-start | bytes 1572872 | tf_op jit(solution)/shard_map/ppermute | solution.py:86
  348.4 36.4 %collective-permute-start.4 = (f32[512,256]{0,1:T(8,128)}, f32[512,256]{0,1:T(8,128)}, u32[]{:S(2)}, u32[]{:S(2)}) collective-permute-start(f32[512,256]{0,1:T(8,128)} %constant_dynamic-slice_fusion.3), channel_id=1, source_target_pairs={{0,1},{1,0},{2,3},{3,2},{4,5},{5,4},{6,7},{7,6},{8,9},{9,8},{10,11... | collective-permute-start | bytes 1572872 | tf_op jit(solution)/shard_map/ppermute | solution.py:86
  354.9 31.0 %collective-permute-start.18 = (f32[256,512]{1,0:T(8,128)}, f32[256,512]{1,0:T(8,128)}, u32[]{:S(2)}, u32[]{:S(2)}) collective-permute-start(f32[256,512]{1,0:T(8,128)} %dynamic-slice_add_fusion), channel_id=1, source_target_pairs={{2,6},{4,0},{3,7},{5,1},{10,14},{12,8},{11,15},{13,9},{18,22},{20,... | collective-permute-start | bytes 1572872 | tf_op jit(solution)/shard_map/ppermute | solution.py:86
  387.4 3.6 collective-permute-start.19
  391.0 5.4 %collective-permute-start.20 = (f32[512]{0:T(512)S(1)}, f32[512]{0:T(512)S(1)}, u32[]{:S(2)}, u32[]{:S(2)}) collective-permute-start(f32[512]{0:T(512)S(1)} %add.212), channel_id=1, source_target_pairs={{6,0},{0,2},{2,4},{4,6},{7,1},{1,3},{3,5},{5,7},{14,8},{8,10},{10,... | collective-permute-start | bytes 6152 | tf_op jit(solution)/shard_map/ppermute | solution.py:19
  391.0 5.4 %collective-permute-start.21 = (f32[512]{0:T(512)S(1)}, f32[512]{0:T(512)S(1)}, u32[]{:S(2)}, u32[]{:S(2)}) collective-permute-start(f32[512]{0:T(512)S(1)} %add.212), channel_id=1, source_target_pairs={{4,0},{6,2},{0,4},{2,6},{5,1},{7,3},{1,5},{3,7},{12,8},{14,10},{8,... | collective-permute-start | bytes 6152 | tf_op jit(solution)/shard_map/ppermute | solution.py:19

commit v2 on v1

--- a/solution.py
+++ b/solution.py
@@ -1,6 +1,8 @@
 import jax
 import jax.numpy as jnp
 from jax import lax
+from jax.experimental import pallas as pl
+from jax.experimental.pallas import tpu as pltpu
 from jax.sharding import PartitionSpec as P
 
 LAG = 240
@@ -79,7 +81,175 @@
     factor = float(BANDS * block_rows)
     return factor * kernel / jnp.sqrt(degree[None, :, None] * column_degrees[:, None, :])
 
-CHUNKS = 2
+CHUNK = 64
+PIECE = 80
+
+
+def gather_kernel(own, before, extra, start, tail, sent, got_before, got_extra, got_start, got_tail):
+    row, slot, here = lax.axis_index("row"), lax.axis_index("col"), lax.axis_index("space")
+    groups = lax.axis_size("row")
+    rows = own.shape[0]
+    first = rows - LAG
+    n_chunk, n_piece = rows // CHUNK, LAG // PIECE
+    barrier = pltpu.get_barrier_semaphore()
+
+    def greet(group, place):
+        pl.semaphore_signal(
+            barrier, inc=1, device_id=(group, place, here), device_id_type=pl.DeviceIdType.MESH
+        )
+
+    def chunk(ref, c):
+        return ref.at[pl.ds(c * CHUNK, CHUNK)]
+
+    def piece(ref, p, offset=0):
+        return ref.at[pl.ds(offset + p * PIECE, PIECE)]
+
+    def copy(src, dst, kind, i, got, group, place):
+        return pltpu.make_async_remote_copy(
+            src_ref=src,
+            dst_ref=dst,
+            send_sem=sent.at[kind, i],
+            recv_sem=got.at[i],
+            device_id=(group, place, here),
+            device_id_type=pl.DeviceIdType.MESH,
+        )
+
+    def send_chunk(src, dst, c, kind, got, place):
+        made = copy(chunk(src, c), chunk(dst, c), kind, c, got, row, place)
+        made.start()
+        return made
+
+    def send_piece(src, dst, p, kind, got, group, place, offset=0):
+        made = copy(piece(src, p, offset), piece(dst, p), kind, p, got, group, place)
+        made.start()
+        return made
+
+    def wait_chunk(dst, c, got):
+        copy(chunk(dst, c), chunk(dst, c), 0, c, got, row, slot).wait_recv()
+
+    def wait_piece(dst, p, got):
+        copy(piece(dst, p), piece(dst, p), 0, p, got, row, slot).wait_recv()
+
+    def all_sent(made):
+        for one in made:
+            one.wait_send()
+
+    @pl.when(slot == 0)
+    def _():
+        greet(row, 1)
+        pl.semaphore_wait(barrier, 1)
+        made = [send_chunk(own, before, c, 0, got_before, 1) for c in range(n_chunk)]
+        for c in range(n_chunk):
+            wait_chunk(extra, c, got_extra)
+        for p in range(n_piece):
+            wait_piece(tail, p, got_tail)
+
+        @pl.when(row > 0)
+        def _():
+            for p in range(n_piece):
+                wait_piece(start, p, got_start)
+
+        all_sent(made)
+
+    @pl.when(slot == 1)
+    def _():
+        greet(row, 0)
+        greet(row, 2)
+        greet(row, 3)
+        pl.semaphore_wait(barrier, 3)
+        made = [send_chunk(own, before, c, 0, got_before, 2) for c in range(n_chunk)]
+        for c in range(n_chunk):
+            wait_chunk(extra, c, got_extra)
+            made.append(send_chunk(extra, extra, c, 1, got_extra, 0))
+            wait_chunk(before, c, got_before)
+            made.append(send_chunk(before, extra, c, 2, got_extra, 2))
+        for p in range(n_piece):
+            wait_piece(tail, p, got_tail)
+            made.append(send_piece(tail, tail, p, 3, got_tail, row, 0))
+
+        @pl.when(row > 0)
+        def _():
+            more = []
+            for p in range(n_piece):
+                wait_piece(start, p, got_start)
+                more.append(send_piece(start, start, p, 4, got_start, row, 0))
+            all_sent(more)
+
+        all_sent(made)
+
+    @pl.when(slot == 2)
+    def _():
+        greet(row, 1)
+        greet(row, 3)
+
+        @pl.when(row > 0)
+        def _():
+            greet(row - 1, 3)
+
+        pl.semaphore_wait(barrier, 2 + (row > 0).astype(jnp.int32))
+        made = [send_chunk(own, before, c, 0, got_before, 3) for c in range(n_chunk)]
+
+        @pl.when(row > 0)
+        def _():
+            more = []
+            for p in range(n_piece):
+                wait_piece(start, p, got_start)
+                more.append(send_piece(start, start, p, 4, got_start, row, 1))
+            all_sent(more)
+
+        made += [send_piece(own, tail, p, 3, got_tail, row, 1, first) for p in range(n_piece)]
+        for c in range(n_chunk):
+            wait_chunk(before, c, got_before)
+        made += [send_piece(before, tail, p, 1, got_tail, row, 3, first) for p in range(n_piece)]
+        for c in range(n_chunk):
+            wait_chunk(extra, c, got_extra)
+        all_sent(made)
+
+    @pl.when(slot == 3)
+    def _():
+        greet(row, 1)
+        greet(row, 2)
+
+        @pl.when(row < groups - 1)
+        def _():
+            greet(row + 1, 2)
+
+        pl.semaphore_wait(barrier, 2 + (row < groups - 1).astype(jnp.int32))
+        made = [send_chunk(own, extra, c, 0, got_extra, 1) for c in range(n_chunk)]
+
+        @pl.when(row < groups - 1)
+        def _():
+            all_sent(
+                [send_piece(own, start, p, 4, got_start, row + 1, 2, first) for p in range(n_piece)]
+            )
+
+        for c in range(n_chunk):
+            wait_chunk(before, c, got_before)
+        for p in range(n_piece):
+            wait_piece(tail, p, got_tail)
+        all_sent(made)
+
+
+def gather_blocks(masked):
+    rows, cells = masked.shape
+    n_chunk, n_piece = rows // CHUNK, LAG // PIECE
+    block = jax.ShapeDtypeStruct((rows, cells), masked.dtype)
+    part = jax.ShapeDtypeStruct((LAG, cells), masked.dtype)
+    anywhere = pl.BlockSpec(memory_space=pl.ANY)
+    return pl.pallas_call(
+        gather_kernel,
+        out_shape=[block, block, part, part],
+        in_specs=[anywhere],
+        out_specs=[anywhere] * 4,
+        scratch_shapes=[
+            pltpu.SemaphoreType.DMA((5, n_chunk)),
+            pltpu.SemaphoreType.DMA((n_chunk,)),
+            pltpu.SemaphoreType.DMA((n_chunk,)),
+            pltpu.SemaphoreType.DMA((n_piece,)),
+            pltpu.SemaphoreType.DMA((n_piece,)),
+        ],
+        compiler_params=pltpu.CompilerParams(collective_id=0, has_side_effects=True),
+    )(masked)
 
 
 def routed(block, axis, pairs):
@@ -102,38 +272,14 @@
     width = block_rows // spaces
     slot = lax.axis_index("col")
     here = lax.axis_index("space")
-    groups = lax.axis_size("row")
     masked = snapshots * ocean_mask.astype(jnp.bfloat16)[None, :]
-    tail = masked[block_rows - LAG :]
-    step = block_rows // CHUNKS
-    chunks = [masked[i * step : (i + 1) * step] for i in range(CHUNKS)]
-
-    start_2 = routed(tail, ("row", "col"), [(4 * (g - 1) + 3, 4 * g + 2) for g in range(1, groups)])
-    tail2_1 = routed(tail, "col", [(2, 1)])
-    before, third, third_on, first_on = [], [], [], []
-    for chunk in chunks:
-        got = routed(chunk, "col", [(0, 1), (1, 2), (2, 3)])
-        far = routed(chunk, "col", [(3, 1)])
-        before.append(got)
-        third.append(far)
-        third_on.append(routed(far, "col", [(1, 0)]))
-        first_on.append(routed(got, "col", [(1, 2)]))
-    start_1 = routed(start_2, "col", [(2, 1)])
-    start_0 = routed(start_1, "col", [(1, 0)])
-    start = start_0 + start_1 + start_2
-    tail2_0 = routed(tail2_1, "col", [(1, 0)])
-    before = jnp.concatenate(before)
-    tail1_3 = routed(before[block_rows - LAG :], "col", [(2, 3)])
-    third = jnp.concatenate(third)
-    third_on = jnp.concatenate(third_on)
-    first_on = jnp.concatenate(first_on)
-
-    rows = jnp.concatenate([pick(slot == 0, start, before[block_rows - LAG :]), masked])
-    next_tail = pick(
-        slot == 1, start, pick(slot == 2, first_on[block_rows - LAG :], tail2_0 + tail1_3)
-    )
-    next_rows = jnp.concatenate([next_tail, before + third_on])
-    last_rows = jnp.concatenate([pick(slot == 1, tail2_1, start), pick(slot == 1, third, first_on)])
+    before, extra, start, tail = gather_blocks(masked)
+    start = pick(lax.axis_index("row") == 0, jnp.zeros_like(start), start)
+    before_tail, extra_tail = before[block_rows - LAG :], extra[block_rows - LAG :]
+    rows = jnp.concatenate([pick(slot == 0, start, before_tail), masked])
+    next_tail = pick(slot == 1, start, pick(slot == 2, extra_tail, tail))
+    next_rows = jnp.concatenate([next_tail, pick(slot == 0, extra, before)])
+    last_rows = jnp.concatenate([pick(slot == 1, tail, start), extra])
 
     over = [(i, 1 - i) for i in range(2)]
 

time: 404 us -> 357 us (0.88)
  waiting for transfers between devices: 273 us -> 11 us
  Pallas kernels: 0 us -> 243 us
  starting transfers between devices: 35.9 us -> 7.72 us
    ppermute x20 -> x6, waiting for transfers between devices: 268 us -> 5.6 us  [routed(): return lax.ppermute(block, axis, pairs)]
    pallas_call x0 -> x1, Pallas kernels: none -> 243 us  [gather_blocks(): pl.pallas_call(gather_kernel, out_shape=[block, block, part, part], in_sp...]
    ppermute x20 -> x6, starting transfers between devices: 35.9 us -> 6.9 us  [routed(): return lax.ppermute(block, axis, pairs)]
    select_n x3 -> x2, other arithmetic: 11.2 us -> 4.7 us  [pick(): return lax.select(jnp.broadcast_to(condition, yes.shape), yes, no)]
  transfers between devices with their start and end apart: 22 -> 8, of which waited for: 12 -> 4; matrix products, arithmetic and copies ran while one was open for 5% -> 13% of each run, Pallas kernels for 0% -> 0%
where the time goes in v2:
time: 357 us; the launch traced here: 353 us
  Pallas kernels  243 us (68%)
  other arithmetic  44.9 us (13%)
  matrix products  22.7 us (6%)
  local copies, waits for them, and re-layouts  21.9 us (6%)
  waiting for transfers between devices  11 us (3%)
  starting transfers between devices  7.72 us (2%)
    pallas_call x1, Pallas kernels, gather_blocks(): pl.pallas_call(gather_kernel, out_shape=[block, block, part, part], in_sp...  243 us
    dot_general x3, matrix products, partial_lagged(): lax.dot_general(rows, columns, (((1,), (1,)), ((), ())), preferred_elemen...  22.7 us
    add x21, other arithmetic, combine_lags(): return earlier[-keep:, -keep:] + later[:keep, :keep]  21.5 us
    slice x9, local copies, waits for them, and re-layouts, combine_lags(): return earlier[-keep:, -keep:] + later[:keep, :keep]  7.73 us
  transfers between devices with their start and end apart: 8, of which 4 were waited for; matrix products, arithmetic and copies ran while one was open for 13% of the time, Pallas kernels for 0%

profile of v2, /device:TPU:2, one launch (start us, length us, event | category | flops | bytes accessed | tf_op | source)
XLA Modules:
  0.0 352.7 jit_solution(7645026005862732278)
XLA Ops:
  0.0 0.7 convert_element_type.12
  0.7 4.4 %broadcast_multiply_fusion.own = bf16[512,4096]{1,0:T(8,128)(2,1)} fusion(bf16[512,4096]{1,0:T(8,128)(2,1)} %param.3, bf16[4096]{0:T(1024)(128)(2,1)S(1)} %convert_element_type.12), kind=kLoop, calls=%fused_computation.30 | loop fusion | flops 2097152 | bytes 8396800 | tf_op jit(solution)/shard_map/mul | solution.py:275
  5.1 243.2 %shard_map.37 = (bf16[512,4096]{1,0:T(8,128)(2,1)}, bf16[512,4096]{1,0:T(8,128)(2,1)}, bf16[240,4096]{1,0:T(8,128)(2,1)}, bf16[240,4096]{1,0:T(8,128)(2,1)}) custom-call(bf16[512,4096]{1,0:T(8,128)(2,1)} %broadcast_multiply_fusion.own), custom_call_target="tpu_custom_call" | custom-call | tf_op jit(solution)/shard_map/pallas_call | solution.py:239
  248.3 2.8 broadcast_select_fusion
  251.1 0.6 copy-done.2
  251.8 1.3 copy-done.9
  253.0 1.4 copy-done.10
  254.5 1.9 select_select_fusion
  256.4 0.8 copy-done
  257.3 1.3 multiply_reduce_fusion.2
  258.5 3.2 multiply_reduce_fusion
  261.7 5.0 %multiply_subtract_fusion = f32[752,752]{1,0:T(8,128)S(1)} fusion(bf16[512,4096]{1,0:T(8,128)(2,1)S(1)} %copy-done.2, bf16[240,4096]{1,0:T(8,128)(2,1)S(1)} %get-tuple-element.14, f32[752]{0:T(1024)S(1)} %get-tuple-element.25, f32[752]{0:T(1024)S(1)} %multiply_reduce_fusion.2, bf16[512,4096]{1,0:T(8,128)(2,1)S(1)} %copy-done, ...), kind=kOutput, calls=%fused_computation.18 | convolution fusion | flops 4658946048 | bytes 14588800 | tf_op jit(solution)/shard_map/dot_general | solution.py:264
  266.7 0.9 slice_add_fusion.2
  267.6 0.8 slice_add_fusion.1
  268.4 0.8 slice_add_fusion
  269.3 0.7 slice_add_fusion.9
  269.9 1.5 slice.335
  271.4 0.6 slice_add_fusion.12
  272.1 1.5 slice.336
  273.6 0.6 slice_add_fusion.15
  274.2 2.1 fusion.15
  276.3 4.5 %fusion.4 = f32[512,512]{1,0:T(8,128)S(1)} fusion(f32[513,513]{1,0:T(8,128)} %get-tuple-element.22, f32[513,513]{1,0:T(8,128)} %get-tuple-element.23, f32[513,513]{1,0:T(8,128)S(1)} %get-tuple-element.21, f32[513,513]{1,0:T(8,128)} %slice.336, f32[513,513]{1,0:T(8,128)} %slice.335), kind=kLoop, calls=%fused_computation.41 | loop fusion | flops 1048576 | bytes 6291456 | tf_op jit(solution)/shard_map/add | solution.py:26
  280.8 0.8 constant_dynamic-slice_fusion
  281.6 1.5 collective-permute-start.3
  283.1 0.9 constant_dynamic-slice_fusion.1
  284.0 0.5 collective-permute-start.2
  284.5 7.5 %multiply_subtract_fusion.1 = f32[752,752]{1,0:T(8,128)S(1)} fusion(bf16[512,4096]{1,0:T(8,128)(2,1)S(1)} %copy-done.4, bf16[240,4096]{1,0:T(8,128)(2,1)} %copy-done.5, f32[752]{0:T(1024)S(1)} %get-tuple-element.26, f32[752]{0:T(1024)S(1)} %multiply_reduce_fusion.2, bf16[512,4096]{1,0:T(8,128)(2,1)S(1)} %copy-done.1, bf16[240,4096]{1,0:T(8,128)(2,1)} %copy-done.6), kind=kOutput, calls=%fused_computation.19 | convolution fusion | flops 4658946048 | bytes 14588800 | tf_op jit(solution)/shard_map/dot_general | solution.py:264
  292.1 0.9 slice_add_fusion.5
  292.9 0.8 slice_add_fusion.4
  293.8 0.8 slice_add_fusion.3
  294.7 0.7 slice_add_fusion.10
  295.7 0.6 slice_add_fusion.13
  296.8 0.6 slice_add_fusion.16
  297.4 0.5 fusion.14
  297.9 1.8 fusion.5
  299.8 0.9 constant_dynamic-slice_fusion.2
  300.9 1.5 collective-permute-start.1
  302.6 2.2 copy.5
  304.9 10.2 %multiply_subtract_fusion.2 = f32[752,752]{0,1:T(8,128)S(1)} fusion(f32[752,752]{0,1:T(8,128)} %copy.5, bf16[512,4096]{1,0:T(8,128)(2,1)} %broadcast_multiply_fusion.own, bf16[240,4096]{1,0:T(8,128)(2,1)} %copy-done.6), kind=kOutput, calls=%fused_computation.20 | convolution fusion | flops 4646060032 | bytes 10684416 | tf_op jit(solution)/shard_map/dot_general | solution.py:264
  315.1 0.8 slice_add_fusion.8
  315.9 0.8 slice_add_fusion.7
  316.8 0.8 slice_add_fusion.6
  317.6 0.7 slice_add_fusion.11
  318.3 0.6 slice_add_fusion.14
  318.9 0.6 slice_add_fusion.17
  319.6 0.5 fusion.13
  320.9 1.8 fusion.6
  322.7 0.8 constant_dynamic-slice_fusion.3
  323.6 0.5 collective-permute-start
  324.8 2.0 dynamic-slice_add_fusion
  326.7 1.3 collective-permute-start.4
  328.0 1.9 dynamic-slice_add_fusion.1
  330.0 1.2 copy.8
  331.2 1.9 add_bitcast_fusion
  333.2 1.2 copy.9
  334.4 1.1 add_bitcast_fusion.1
  335.5 3.5 collective-permute-done.4
  339.1 1.1 fusion.7
  340.5 1.6 collective-permute-start.5
  342.1 2.1 collective-permute-done.5
  344.1 0.8 collective-permute-start.7
  345.0 3.7 %collective-permute-done.7 = f32[512]{0:T(512)S(1)} collective-permute-done((f32[512]{0:T(512)S(1)}, f32[512]{0:T(512)S(1)}, u32[]{:S(2)}, u32[]{:S(2)}) %collective-permute-start.7) | collective-permute-done | bytes 2080 | tf_op jit(solution)/shard_map/ppermute | solution.py:21
  348.6 1.7 collective-permute-done.6
  350.9 1.6 copy.10
  (32 shorter events, 3.0 us)
Async XLA Ops:
  248.3 3.5 copy-start.2
  248.3 4.7 %copy-start.9 = (bf16[240,4096]{1,0:T(8,128)(2,1)S(1)}, bf16[240,4096]{1,0:T(8,128)(2,1)}, u32[]{:S(2)}) copy-start(bf16[240,4096]{1,0:T(8,128)(2,1)} %get-tuple-element.9) | copy-start | bytes 5898244
  248.3 6.2 %copy-start.10 = (bf16[240,4096]{1,0:T(8,128)(2,1)S(1)}, bf16[240,4096]{1,0:T(8,128)(2,1)}, u32[]{:S(2)}) copy-start(bf16[240,4096]{1,0:T(8,128)(2,1)} %get-tuple-element.12) | copy-start | bytes 5898244
  251.1 7.4 %copy-start.3 = (bf16[512,4096]{1,0:T(8,128)(2,1)}, bf16[512,4096]{1,0:T(8,128)(2,1)S(1)}, u32[]{:S(2)}) copy-start(bf16[512,4096]{1,0:T(8,128)(2,1)S(1)} %broadcast_select_fusion) | copy-start | bytes 12582916
  254.5 2.8 copy-start
  256.4 2.1 copy-start.5
  256.4 5.3 %copy-start.6 = (bf16[240,4096]{1,0:T(8,128)(2,1)}, bf16[240,4096]{1,0:T(8,128)(2,1)S(1)}, u32[]{:S(2)}) copy-start(bf16[240,4096]{1,0:T(8,128)(2,1)S(1)} %get-tuple-element.24) | copy-start | bytes 5898244
  276.3 8.2 %copy-start.1 = (bf16[512,4096]{1,0:T(8,128)(2,1)S(1)}, bf16[512,4096]{1,0:T(8,128)(2,1)}, u32[]{:S(2)}) copy-start(bf16[512,4096]{1,0:T(8,128)(2,1)} %broadcast_multiply_fusion.own) | copy-start | bytes 12582916
  276.3 8.2 %copy-start.4 = (bf16[512,4096]{1,0:T(8,128)(2,1)S(1)}, bf16[512,4096]{1,0:T(8,128)(2,1)}, u32[]{:S(2)}) copy-start(bf16[512,4096]{1,0:T(8,128)(2,1)} %copy-done.3) | copy-start | bytes 12582916
  281.6 43.1 %collective-permute-start.3 = (f32[256,512]{1,0:T(8,128)}, f32[256,512]{1,0:T(8,128)}, u32[]{:S(2)}, u32[]{:S(2)}) collective-permute-start(f32[256,512]{1,0:T(8,128)} %constant_dynamic-slice_fusion), channel_id=1, source_target_pairs={{0,1},{1,0},{2,3},{3,2},{4,5},{5,4},{6,7},{7,6},{8,9},{9,8},{10,11... | collective-permute-start | bytes 1572872 | tf_op jit(solution)/shard_map/ppermute | solution.py:256
  284.0 44.0 %collective-permute-start.2 = (f32[512,256]{1,0:T(8,128)}, f32[512,256]{1,0:T(8,128)}, u32[]{:S(2)}, u32[]{:S(2)}) collective-permute-start(f32[512,256]{1,0:T(8,128)} %constant_dynamic-slice_fusion.1), channel_id=1, source_target_pairs={{0,1},{1,0},{2,3},{3,2},{4,5},{5,4},{6,7},{7,6},{8,9},{9,8},{10,11... | collective-permute-start | bytes 1572872 | tf_op jit(solution)/shard_map/ppermute | solution.py:256
  299.8 1.1 copy-start.7
  300.9 30.3 %collective-permute-start.1 = (f32[512,256]{1,0:T(8,128)}, f32[512,256]{1,0:T(8,128)}, u32[]{:S(2)}, u32[]{:S(2)}) collective-permute-start(f32[512,256]{1,0:T(8,128)} %constant_dynamic-slice_fusion.2), channel_id=1, source_target_pairs={{0,1},{1,0},{2,3},{3,2},{4,5},{5,4},{6,7},{7,6},{8,9},{9,8},{10,11... | collective-permute-start | bytes 1572872 | tf_op jit(solution)/shard_map/ppermute | solution.py:256
  323.6 7.7 %copy-start.8 = (f32[512,512]{1,0:T(8,128)S(1)}, f32[512,512]{1,0:T(8,128)}, u32[]{:S(2)}) copy-start(f32[512,512]{1,0:T(8,128)} %copy-done.7) | copy-start | bytes 3145732
  323.6 10.8 %collective-permute-start = (f32[512,256]{0,1:T(8,128)}, f32[512,256]{0,1:T(8,128)}, u32[]{:S(2)}, u32[]{:S(2)}) collective-permute-start(f32[512,256]{0,1:T(8,128)} %constant_dynamic-slice_fusion.3), channel_id=1, source_target_pairs={{0,1},{1,0},{2,3},{3,2},{4,5},{5,4},{6,7},{7,6},{8,9},{9,8},{10,11... | collective-permute-start | bytes 1572872 | tf_op jit(solution)/shard_map/ppermute | solution.py:256
  326.7 12.3 %collective-permute-start.4 = (f32[256,512]{1,0:T(8,128)}, f32[256,512]{1,0:T(8,128)}, u32[]{:S(2)}, u32[]{:S(2)}) collective-permute-start(f32[256,512]{1,0:T(8,128)} %dynamic-slice_add_fusion), channel_id=1, source_target_pairs={{2,6},{4,0},{3,7},{5,1},{10,14},{12,8},{11,15},{13,9},{18,22},{20,... | collective-permute-start | bytes 1572872 | tf_op jit(solution)/shard_map/ppermute | solution.py:256
  340.5 3.6 %collective-permute-start.5 = (f32[512]{0:T(512)S(1)}, f32[512]{0:T(512)S(1)}, u32[]{:S(2)}, u32[]{:S(2)}) collective-permute-start(f32[512]{0:T(512)S(1)} %fusion.12), channel_id=1, source_target_pairs={{0,1},{1,0},{2,3},{3,2},{4,5},{5,4},{6,7},{7,6},{8,9},{9,8},{10,11... | collective-permute-start | bytes 6152 | tf_op jit(solution)/shard_map/ppermute | solution.py:256
  344.1 4.5 %collective-permute-start.7 = (f32[512]{0:T(512)S(1)}, f32[512]{0:T(512)S(1)}, u32[]{:S(2)}, u32[]{:S(2)}) collective-permute-start(f32[512]{0:T(512)S(1)} %add.196), channel_id=1, source_target_pairs={{4,0},{6,2},{0,4},{2,6},{5,1},{7,3},{1,5},{3,7},{12,8},{14,10},{8,... | collective-permute-start | bytes 6152 | tf_op jit(solution)/shard_map/ppermute | solution.py:21
  345.0 5.4 %collective-permute-start.6 = (f32[512]{0:T(512)S(1)}, f32[512]{0:T(512)S(1)}, u32[]{:S(2)}, u32[]{:S(2)}) collective-permute-start(f32[512]{0:T(512)S(1)} %add.196), channel_id=1, source_target_pairs={{6,0},{0,2},{2,4},{4,6},{7,1},{1,3},{3,5},{5,7},{14,8},{8,10},{10,... | collective-permute-start | bytes 6152 | tf_op jit(solution)/shard_map/ppermute | solution.py:21

commit v3 on v2

--- a/solution.py
+++ b/solution.py
@@ -163,9 +163,10 @@
             made.append(send_chunk(extra, extra, c, 1, got_extra, 0))
             wait_chunk(before, c, got_before)
             made.append(send_chunk(before, extra, c, 2, got_extra, 2))
-        for p in range(n_piece):
-            wait_piece(tail, p, got_tail)
-            made.append(send_piece(tail, tail, p, 3, got_tail, row, 0))
+            p = (c - 3) // 2
+            if c % 2 == 1 and 0 <= p < n_piece:
+                wait_piece(tail, p, got_tail)
+                made.append(send_piece(tail, tail, p, 3, got_tail, row, 0))
 
         @pl.when(row > 0)
         def _():
@@ -187,22 +188,26 @@
             greet(row - 1, 3)
 
         pl.semaphore_wait(barrier, 2 + (row > 0).astype(jnp.int32))
-        made = [send_chunk(own, before, c, 0, got_before, 3) for c in range(n_chunk)]
-
-        @pl.when(row > 0)
-        def _():
-            more = []
+        made = [send_piece(own, tail, p, 3, got_tail, row, 1, first) for p in range(n_piece)]
+        made += [send_chunk(own, before, c, 0, got_before, 3) for c in range(n_chunk)]
+
+        @pl.when(row > 0)
+        def _():
             for p in range(n_piece):
                 wait_piece(start, p, got_start)
-                more.append(send_piece(start, start, p, 4, got_start, row, 1))
-            all_sent(more)
-
-        made += [send_piece(own, tail, p, 3, got_tail, row, 1, first) for p in range(n_piece)]
+                send_piece(start, start, p, 4, got_start, row, 1)
+
         for c in range(n_chunk):
             wait_chunk(before, c, got_before)
         made += [send_piece(before, tail, p, 1, got_tail, row, 3, first) for p in range(n_piece)]
         for c in range(n_chunk):
             wait_chunk(extra, c, got_extra)
+
+        @pl.when(row > 0)
+        def _():
+            for p in range(n_piece):
+                copy(piece(start, p), piece(start, p), 4, p, got_start, row, 1).wait_send()
+
         all_sent(made)
 
     @pl.when(slot == 3)

time: 357 us -> 356 us (level)
  transfers between devices with their start and end apart: 8 -> 8, of which waited for: 4 -> 5; matrix products, arithmetic and copies ran while one was open for 13% -> 13% of each run, Pallas kernels for 0% -> 0%
where the time goes in v3:
time: 356 us; the launch traced here: 352 us
  Pallas kernels  240 us (67%)
  other arithmetic  44.9 us (13%)
  matrix products  22.7 us (6%)
  local copies, waits for them, and re-layouts  21.9 us (6%)
  waiting for transfers between devices  14.1 us (4%)
  starting transfers between devices  6.82 us (2%)
    pallas_call x1, Pallas kernels, gather_blocks(): pl.pallas_call(gather_kernel, out_shape=[block, block, part, part], in_sp...  240 us
    dot_general x3, matrix products, partial_lagged(): lax.dot_general(rows, columns, (((1,), (1,)), ((), ())), preferred_elemen...  22.7 us
    add x21, other arithmetic, combine_lags(): return earlier[-keep:, -keep:] + later[:keep, :keep]  21.5 us
    ppermute x6, waiting for transfers between devices, routed(): return lax.ppermute(block, axis, pairs)  8.76 us
    slice x9, local copies, waits for them, and re-layouts, combine_lags(): return earlier[-keep:, -keep:] + later[:keep, :keep]  7.73 us
  transfers between devices with their start and end apart: 8, of which 5 were waited for; matrix products, arithmetic and copies ran while one was open for 13% of the time, Pallas kernels for 0%

profile of v3, /device:TPU:2, one launch (start us, length us, event | category | flops | bytes accessed | tf_op | source)
XLA Modules:
  0.0 352.0 jit_solution(53418567067026712)
XLA Ops:
  0.0 0.7 convert_element_type.12
  0.7 4.4 %broadcast_multiply_fusion.own = bf16[512,4096]{1,0:T(8,128)(2,1)} fusion(bf16[512,4096]{1,0:T(8,128)(2,1)} %param.3, bf16[4096]{0:T(1024)(128)(2,1)S(1)} %convert_element_type.12), kind=kLoop, calls=%fused_computation.30 | loop fusion | flops 2097152 | bytes 8396800 | tf_op jit(solution)/shard_map/mul | solution.py:280
  5.1 240.3 %shard_map.37 = (bf16[512,4096]{1,0:T(8,128)(2,1)}, bf16[512,4096]{1,0:T(8,128)(2,1)}, bf16[240,4096]{1,0:T(8,128)(2,1)}, bf16[240,4096]{1,0:T(8,128)(2,1)}) custom-call(bf16[512,4096]{1,0:T(8,128)(2,1)} %broadcast_multiply_fusion.own), custom_call_target="tpu_custom_call" | custom-call | tf_op jit(solution)/shard_map/pallas_call | solution.py:244
  245.4 2.8 broadcast_select_fusion
  248.2 0.6 copy-done.2
  248.9 1.3 copy-done.9
  250.1 1.4 copy-done.10
  251.6 1.9 select_select_fusion
  253.5 0.8 copy-done
  254.4 1.3 multiply_reduce_fusion.2
  255.6 3.2 multiply_reduce_fusion
  258.8 5.0 %multiply_subtract_fusion = f32[752,752]{1,0:T(8,128)S(1)} fusion(bf16[512,4096]{1,0:T(8,128)(2,1)S(1)} %copy-done.2, bf16[240,4096]{1,0:T(8,128)(2,1)S(1)} %get-tuple-element.14, f32[752]{0:T(1024)S(1)} %get-tuple-element.25, f32[752]{0:T(1024)S(1)} %multiply_reduce_fusion.2, bf16[512,4096]{1,0:T(8,128)(2,1)S(1)} %copy-done, ...), kind=kOutput, calls=%fused_computation.18 | convolution fusion | flops 4658946048 | bytes 14588800 | tf_op jit(solution)/shard_map/dot_general | solution.py:269
  263.8 0.9 slice_add_fusion.2
  264.7 0.8 slice_add_fusion.1
  265.5 0.8 slice_add_fusion
  266.4 0.7 slice_add_fusion.9
  267.0 1.5 slice.335
  268.5 0.6 slice_add_fusion.12
  269.2 1.5 slice.336
  270.7 0.6 slice_add_fusion.15
  271.3 2.1 fusion.15
  273.4 4.5 %fusion.4 = f32[512,512]{1,0:T(8,128)S(1)} fusion(f32[513,513]{1,0:T(8,128)} %get-tuple-element.22, f32[513,513]{1,0:T(8,128)} %get-tuple-element.23, f32[513,513]{1,0:T(8,128)S(1)} %get-tuple-element.21, f32[513,513]{1,0:T(8,128)} %slice.336, f32[513,513]{1,0:T(8,128)} %slice.335), kind=kLoop, calls=%fused_computation.41 | loop fusion | flops 1048576 | bytes 6291456 | tf_op jit(solution)/shard_map/add | solution.py:26
  277.9 0.8 constant_dynamic-slice_fusion
  278.7 1.5 collective-permute-start.3
  280.2 0.9 constant_dynamic-slice_fusion.1
  281.1 0.5 collective-permute-start.2
  281.6 7.5 %multiply_subtract_fusion.1 = f32[752,752]{1,0:T(8,128)S(1)} fusion(bf16[512,4096]{1,0:T(8,128)(2,1)S(1)} %copy-done.4, bf16[240,4096]{1,0:T(8,128)(2,1)} %copy-done.5, f32[752]{0:T(1024)S(1)} %get-tuple-element.26, f32[752]{0:T(1024)S(1)} %multiply_reduce_fusion.2, bf16[512,4096]{1,0:T(8,128)(2,1)S(1)} %copy-done.1, bf16[240,4096]{1,0:T(8,128)(2,1)} %copy-done.6), kind=kOutput, calls=%fused_computation.19 | convolution fusion | flops 4658946048 | bytes 14588800 | tf_op jit(solution)/shard_map/dot_general | solution.py:269
  289.2 0.9 slice_add_fusion.5
  290.0 0.8 slice_add_fusion.4
  290.9 0.8 slice_add_fusion.3
  291.7 0.7 slice_add_fusion.10
  292.8 0.6 slice_add_fusion.13
  293.9 0.6 slice_add_fusion.16
  294.5 0.5 fusion.14
  295.0 1.8 fusion.5
  296.9 0.9 constant_dynamic-slice_fusion.2
  298.0 1.5 collective-permute-start.1
  299.7 2.2 copy.5
  301.9 10.2 %multiply_subtract_fusion.2 = f32[752,752]{0,1:T(8,128)S(1)} fusion(f32[752,752]{0,1:T(8,128)} %copy.5, bf16[512,4096]{1,0:T(8,128)(2,1)} %broadcast_multiply_fusion.own, bf16[240,4096]{1,0:T(8,128)(2,1)} %copy-done.6), kind=kOutput, calls=%fused_computation.20 | convolution fusion | flops 4646060032 | bytes 10684416 | tf_op jit(solution)/shard_map/dot_general | solution.py:269
  312.2 0.8 slice_add_fusion.8
  313.0 0.8 slice_add_fusion.7
  313.9 0.8 slice_add_fusion.6
  314.7 0.7 slice_add_fusion.11
  315.4 0.6 slice_add_fusion.14
  316.0 0.6 slice_add_fusion.17
  316.7 0.5 fusion.13
  318.0 1.8 fusion.6
  319.8 0.8 constant_dynamic-slice_fusion.3
  320.7 0.5 collective-permute-start
  321.8 2.0 dynamic-slice_add_fusion
  323.8 1.3 collective-permute-start.4
  325.1 1.9 dynamic-slice_add_fusion.1
  327.1 1.2 copy.8
  328.3 1.9 add_bitcast_fusion
  330.2 1.2 copy.9
  331.5 2.0 collective-permute-done
  333.5 1.1 add_bitcast_fusion.1
  334.6 4.6 %collective-permute-done.4 = f32[256,512]{1,0:T(8,128)} collective-permute-done((f32[256,512]{1,0:T(8,128)}, f32[256,512]{1,0:T(8,128)}, u32[]{:S(2)}, u32[]{:S(2)}) %collective-permute-start.4) | collective-permute-done | bytes 524320 | tf_op jit(solution)/shard_map/ppermute | solution.py:261
  339.2 1.1 fusion.7
  340.7 1.5 collective-permute-start.5
  342.1 2.2 collective-permute-done.5
  344.3 4.5 %collective-permute-done.7 = f32[512]{0:T(512)S(1)} collective-permute-done((f32[512]{0:T(512)S(1)}, f32[512]{0:T(512)S(1)}, u32[]{:S(2)}, u32[]{:S(2)}) %collective-permute-start.7) | collective-permute-done | bytes 2080 | tf_op jit(solution)/shard_map/ppermute | solution.py:21
  348.8 0.9 collective-permute-done.6
  350.2 1.6 copy.10
  (32 shorter events, 2.9 us)
Async XLA Ops:
  245.4 3.5 copy-start.2
  245.4 4.7 %copy-start.9 = (bf16[240,4096]{1,0:T(8,128)(2,1)S(1)}, bf16[240,4096]{1,0:T(8,128)(2,1)}, u32[]{:S(2)}) copy-start(bf16[240,4096]{1,0:T(8,128)(2,1)} %get-tuple-element.9) | copy-start | bytes 5898244
  245.4 6.2 %copy-start.10 = (bf16[240,4096]{1,0:T(8,128)(2,1)S(1)}, bf16[240,4096]{1,0:T(8,128)(2,1)}, u32[]{:S(2)}) copy-start(bf16[240,4096]{1,0:T(8,128)(2,1)} %get-tuple-element.12) | copy-start | bytes 5898244
  248.2 7.4 %copy-start.3 = (bf16[512,4096]{1,0:T(8,128)(2,1)}, bf16[512,4096]{1,0:T(8,128)(2,1)S(1)}, u32[]{:S(2)}) copy-start(bf16[512,4096]{1,0:T(8,128)(2,1)S(1)} %broadcast_select_fusion) | copy-start | bytes 12582916
  251.6 2.8 copy-start
  253.5 2.1 copy-start.5
  253.5 5.3 %copy-start.6 = (bf16[240,4096]{1,0:T(8,128)(2,1)}, bf16[240,4096]{1,0:T(8,128)(2,1)S(1)}, u32[]{:S(2)}) copy-start(bf16[240,4096]{1,0:T(8,128)(2,1)S(1)} %get-tuple-element.24) | copy-start | bytes 5898244
  273.4 8.2 %copy-start.1 = (bf16[512,4096]{1,0:T(8,128)(2,1)S(1)}, bf16[512,4096]{1,0:T(8,128)(2,1)}, u32[]{:S(2)}) copy-start(bf16[512,4096]{1,0:T(8,128)(2,1)} %broadcast_multiply_fusion.own) | copy-start | bytes 12582916
  273.4 8.2 %copy-start.4 = (bf16[512,4096]{1,0:T(8,128)(2,1)S(1)}, bf16[512,4096]{1,0:T(8,128)(2,1)}, u32[]{:S(2)}) copy-start(bf16[512,4096]{1,0:T(8,128)(2,1)} %copy-done.3) | copy-start | bytes 12582916
  278.7 43.1 %collective-permute-start.3 = (f32[256,512]{1,0:T(8,128)}, f32[256,512]{1,0:T(8,128)}, u32[]{:S(2)}, u32[]{:S(2)}) collective-permute-start(f32[256,512]{1,0:T(8,128)} %constant_dynamic-slice_fusion), channel_id=1, source_target_pairs={{0,1},{1,0},{2,3},{3,2},{4,5},{5,4},{6,7},{7,6},{8,9},{9,8},{10,11... | collective-permute-start | bytes 1572872 | tf_op jit(solution)/shard_map/ppermute | solution.py:261
  281.1 44.0 %collective-permute-start.2 = (f32[512,256]{1,0:T(8,128)}, f32[512,256]{1,0:T(8,128)}, u32[]{:S(2)}, u32[]{:S(2)}) collective-permute-start(f32[512,256]{1,0:T(8,128)} %constant_dynamic-slice_fusion.1), channel_id=1, source_target_pairs={{0,1},{1,0},{2,3},{3,2},{4,5},{5,4},{6,7},{7,6},{8,9},{9,8},{10,11... | collective-permute-start | bytes 1572872 | tf_op jit(solution)/shard_map/ppermute | solution.py:261
  296.8 1.1 copy-start.7
  298.0 30.3 %collective-permute-start.1 = (f32[512,256]{1,0:T(8,128)}, f32[512,256]{1,0:T(8,128)}, u32[]{:S(2)}, u32[]{:S(2)}) collective-permute-start(f32[512,256]{1,0:T(8,128)} %constant_dynamic-slice_fusion.2), channel_id=1, source_target_pairs={{0,1},{1,0},{2,3},{3,2},{4,5},{5,4},{6,7},{7,6},{8,9},{9,8},{10,11... | collective-permute-start | bytes 1572872 | tf_op jit(solution)/shard_map/ppermute | solution.py:261
  320.7 7.6 %copy-start.8 = (f32[512,512]{1,0:T(8,128)S(1)}, f32[512,512]{1,0:T(8,128)}, u32[]{:S(2)}) copy-start(f32[512,512]{1,0:T(8,128)} %copy-done.7) | copy-start | bytes 3145732
  320.7 12.8 %collective-permute-start = (f32[512,256]{0,1:T(8,128)}, f32[512,256]{0,1:T(8,128)}, u32[]{:S(2)}, u32[]{:S(2)}) collective-permute-start(f32[512,256]{0,1:T(8,128)} %constant_dynamic-slice_fusion.3), channel_id=1, source_target_pairs={{0,1},{1,0},{2,3},{3,2},{4,5},{5,4},{6,7},{7,6},{8,9},{9,8},{10,11... | collective-permute-start | bytes 1572872 | tf_op jit(solution)/shard_map/ppermute | solution.py:261
  323.8 15.4 %collective-permute-start.4 = (f32[256,512]{1,0:T(8,128)}, f32[256,512]{1,0:T(8,128)}, u32[]{:S(2)}, u32[]{:S(2)}) collective-permute-start(f32[256,512]{1,0:T(8,128)} %dynamic-slice_add_fusion), channel_id=1, source_target_pairs={{2,6},{4,0},{3,7},{5,1},{10,14},{12,8},{11,15},{13,9},{18,22},{20,... | collective-permute-start | bytes 1572872 | tf_op jit(solution)/shard_map/ppermute | solution.py:261
  340.7 3.6 %collective-permute-start.5 = (f32[512]{0:T(512)S(1)}, f32[512]{0:T(512)S(1)}, u32[]{:S(2)}, u32[]{:S(2)}) collective-permute-start(f32[512]{0:T(512)S(1)} %fusion.12), channel_id=1, source_target_pairs={{0,1},{1,0},{2,3},{3,2},{4,5},{5,4},{6,7},{7,6},{8,9},{9,8},{10,11... | collective-permute-start | bytes 6152 | tf_op jit(solution)/shard_map/ppermute | solution.py:261
  344.3 4.5 %collective-permute-start.7 = (f32[512]{0:T(512)S(1)}, f32[512]{0:T(512)S(1)}, u32[]{:S(2)}, u32[]{:S(2)}) collective-permute-start(f32[512]{0:T(512)S(1)} %add.196), channel_id=1, source_target_pairs={{4,0},{6,2},{0,4},{2,6},{5,1},{7,3},{1,5},{3,7},{12,8},{14,10},{8,... | collective-permute-start | bytes 6152 | tf_op jit(solution)/shard_map/ppermute | solution.py:21
  344.3 5.4 %collective-permute-start.6 = (f32[512]{0:T(512)S(1)}, f32[512]{0:T(512)S(1)}, u32[]{:S(2)}, u32[]{:S(2)}) collective-permute-start(f32[512]{0:T(512)S(1)} %add.196), channel_id=1, source_target_pairs={{6,0},{0,2},{2,4},{4,6},{7,1},{1,3},{3,5},{5,7},{14,8},{8,10},{10,... | collective-permute-start | bytes 6152 | tf_op jit(solution)/shard_map/ppermute | solution.py:21

commit v4 on v3

--- a/solution.py
+++ b/solution.py
@@ -158,23 +158,31 @@
         greet(row, 3)
         pl.semaphore_wait(barrier, 3)
         made = [send_chunk(own, before, c, 0, got_before, 2) for c in range(n_chunk)]
-        for c in range(n_chunk):
-            wait_chunk(extra, c, got_extra)
-            made.append(send_chunk(extra, extra, c, 1, got_extra, 0))
-            wait_chunk(before, c, got_before)
-            made.append(send_chunk(before, extra, c, 2, got_extra, 2))
-            p = (c - 3) // 2
-            if c % 2 == 1 and 0 <= p < n_piece:
-                wait_piece(tail, p, got_tail)
-                made.append(send_piece(tail, tail, p, 3, got_tail, row, 0))
-
-        @pl.when(row > 0)
-        def _():
-            more = []
-            for p in range(n_piece):
-                wait_piece(start, p, got_start)
-                more.append(send_piece(start, start, p, 4, got_start, row, 0))
-            all_sent(more)
+        turns = [((c + 1) * 11, 0, c) for c in range(n_chunk)]
+        turns += [((c + 1) * 20, 1, c) for c in range(n_chunk)]
+        turns += [((p + 1) * 30, 2, p) for p in range(n_piece)]
+        turns += [(110 + p * 20, 3, p) for p in range(n_piece)]
+        for _, kind, i in sorted(turns):
+            if kind == 0:
+                wait_chunk(before, i, got_before)
+                made.append(send_chunk(before, extra, i, 2, got_extra, 2))
+            elif kind == 1:
+                wait_chunk(extra, i, got_extra)
+                made.append(send_chunk(extra, extra, i, 1, got_extra, 0))
+            elif kind == 2:
+                wait_piece(tail, i, got_tail)
+                made.append(send_piece(tail, tail, i, 3, got_tail, row, 0))
+            else:
+
+                @pl.when(row > 0)
+                def _():
+                    wait_piece(start, i, got_start)
+                    send_piece(start, start, i, 4, got_start, row, 0)
+
+        @pl.when(row > 0)
+        def _():
+            for p in range(n_piece):
+                copy(piece(start, p), piece(start, p), 4, p, got_start, row, 0).wait_send()
 
         all_sent(made)
 
@@ -220,18 +228,26 @@
             greet(row + 1, 2)
 
         pl.semaphore_wait(barrier, 2 + (row < groups - 1).astype(jnp.int32))
-        made = [send_chunk(own, extra, c, 0, got_extra, 1) for c in range(n_chunk)]
+        made = [send_chunk(own, extra, c, 0, got_extra, 1) for c in range(2)]
 
         @pl.when(row < groups - 1)
         def _():
-            all_sent(
-                [send_piece(own, start, p, 4, got_start, row + 1, 2, first) for p in range(n_piece)]
-            )
+            for p in range(n_piece):
+                send_piece(own, start, p, 4, got_start, row + 1, 2, first)
+
+        made += [send_chunk(own, extra, c, 0, got_extra, 1) for c in range(2, n_chunk)]
 
         for c in range(n_chunk):
             wait_chunk(before, c, got_before)
         for p in range(n_piece):
             wait_piece(tail, p, got_tail)
+
+        @pl.when(row < groups - 1)
+        def _():
+            for p in range(n_piece):
+                last = piece(own, p, first)
+                copy(last, piece(start, p), 4, p, got_start, row + 1, 2).wait_send()
+
         all_sent(made)
 
 

time: 356 us -> 367 us (1.031)
  Pallas kernels: 240 us -> 252 us
    pallas_call x1, Pallas kernels: 240 us -> 252 us  [gather_blocks(): pl.pallas_call(gather_kernel, out_shape=[block, block, part, part], in_sp...]
where the time goes in v4:
time: 367 us; the launch traced here: 363 us
  Pallas kernels  252 us (69%)
  other arithmetic  44.9 us (12%)
  matrix products  22.7 us (6%)
  local copies, waits for them, and re-layouts  21.9 us (6%)
  waiting for transfers between devices  14.1 us (4%)
  starting transfers between devices  6.82 us (2%)
    pallas_call x1, Pallas kernels, gather_blocks(): pl.pallas_call(gather_kernel, out_shape=[block, block, part, part], in_sp...  252 us
    dot_general x3, matrix products, partial_lagged(): lax.dot_general(rows, columns, (((1,), (1,)), ((), ())), preferred_elemen...  22.7 us
    add x21, other arithmetic, combine_lags(): return earlier[-keep:, -keep:] + later[:keep, :keep]  21.5 us
    ppermute x6, waiting for transfers between devices, routed(): return lax.ppermute(block, axis, pairs)  8.76 us
    slice x9, local copies, waits for them, and re-layouts, combine_lags(): return earlier[-keep:, -keep:] + later[:keep, :keep]  7.73 us
  transfers between devices with their start and end apart: 8, of which 5 were waited for; matrix products, arithmetic and copies ran while one was open for 13% of the time, Pallas kernels for 0%

profile of v4, /device:TPU:2, one launch (start us, length us, event | category | flops | bytes accessed | tf_op | source)
XLA Modules:
  0.0 363.3 jit_solution(1532849139683382752)
XLA Ops:
  0.0 0.7 convert_element_type.12
  0.7 4.4 %broadcast_multiply_fusion.own = bf16[512,4096]{1,0:T(8,128)(2,1)} fusion(bf16[512,4096]{1,0:T(8,128)(2,1)} %param.3, bf16[4096]{0:T(1024)(128)(2,1)S(1)} %convert_element_type.12), kind=kLoop, calls=%fused_computation.30 | loop fusion | flops 2097152 | bytes 8396800 | tf_op jit(solution)/shard_map/mul | solution.py:296
  5.1 251.5 %shard_map.37 = (bf16[512,4096]{1,0:T(8,128)(2,1)}, bf16[512,4096]{1,0:T(8,128)(2,1)}, bf16[240,4096]{1,0:T(8,128)(2,1)}, bf16[240,4096]{1,0:T(8,128)(2,1)}) custom-call(bf16[512,4096]{1,0:T(8,128)(2,1)} %broadcast_multiply_fusion.own), custom_call_target="tpu_custom_call" | custom-call | tf_op jit(solution)/shard_map/pallas_call | solution.py:260
  256.7 2.8 broadcast_select_fusion
  259.5 0.6 copy-done.2
  260.1 1.3 copy-done.9
  261.4 1.4 copy-done.10
  262.8 1.9 select_select_fusion
  264.8 0.8 copy-done
  265.6 1.3 multiply_reduce_fusion.2
  266.9 3.2 multiply_reduce_fusion
  270.1 5.0 %multiply_subtract_fusion = f32[752,752]{1,0:T(8,128)S(1)} fusion(bf16[512,4096]{1,0:T(8,128)(2,1)S(1)} %copy-done.2, bf16[240,4096]{1,0:T(8,128)(2,1)S(1)} %get-tuple-element.14, f32[752]{0:T(1024)S(1)} %get-tuple-element.25, f32[752]{0:T(1024)S(1)} %multiply_reduce_fusion.2, bf16[512,4096]{1,0:T(8,128)(2,1)S(1)} %copy-done, ...), kind=kOutput, calls=%fused_computation.18 | convolution fusion | flops 4658946048 | bytes 14588800 | tf_op jit(solution)/shard_map/dot_general | solution.py:285
  275.0 0.9 slice_add_fusion.2
  275.9 0.8 slice_add_fusion.1
  276.8 0.8 slice_add_fusion
  277.6 0.7 slice_add_fusion.9
  278.3 1.5 slice.335
  279.8 0.6 slice_add_fusion.12
  280.4 1.5 slice.336
  281.9 0.6 slice_add_fusion.15
  282.6 2.1 fusion.15
  284.7 4.5 %fusion.4 = f32[512,512]{1,0:T(8,128)S(1)} fusion(f32[513,513]{1,0:T(8,128)} %get-tuple-element.22, f32[513,513]{1,0:T(8,128)} %get-tuple-element.23, f32[513,513]{1,0:T(8,128)S(1)} %get-tuple-element.21, f32[513,513]{1,0:T(8,128)} %slice.336, f32[513,513]{1,0:T(8,128)} %slice.335), kind=kLoop, calls=%fused_computation.41 | loop fusion | flops 1048576 | bytes 6291456 | tf_op jit(solution)/shard_map/add | solution.py:26
  289.1 0.8 constant_dynamic-slice_fusion
  290.0 1.5 collective-permute-start.3
  291.5 0.9 constant_dynamic-slice_fusion.1
  292.4 0.5 collective-permute-start.2
  292.9 7.5 %multiply_subtract_fusion.1 = f32[752,752]{1,0:T(8,128)S(1)} fusion(bf16[512,4096]{1,0:T(8,128)(2,1)S(1)} %copy-done.4, bf16[240,4096]{1,0:T(8,128)(2,1)} %copy-done.5, f32[752]{0:T(1024)S(1)} %get-tuple-element.26, f32[752]{0:T(1024)S(1)} %multiply_reduce_fusion.2, bf16[512,4096]{1,0:T(8,128)(2,1)S(1)} %copy-done.1, bf16[240,4096]{1,0:T(8,128)(2,1)} %copy-done.6), kind=kOutput, calls=%fused_computation.19 | convolution fusion | flops 4658946048 | bytes 14588800 | tf_op jit(solution)/shard_map/dot_general | solution.py:285
  300.4 0.9 slice_add_fusion.5
  301.3 0.8 slice_add_fusion.4
  302.1 0.8 slice_add_fusion.3
  303.0 0.7 slice_add_fusion.10
  304.1 0.6 slice_add_fusion.13
  305.1 0.6 slice_add_fusion.16
  305.8 0.5 fusion.14
  306.3 1.8 fusion.5
  308.1 0.9 constant_dynamic-slice_fusion.2
  309.2 1.5 collective-permute-start.1
  311.0 2.2 copy.5
  313.2 10.2 %multiply_subtract_fusion.2 = f32[752,752]{0,1:T(8,128)S(1)} fusion(f32[752,752]{0,1:T(8,128)} %copy.5, bf16[512,4096]{1,0:T(8,128)(2,1)} %broadcast_multiply_fusion.own, bf16[240,4096]{1,0:T(8,128)(2,1)} %copy-done.6), kind=kOutput, calls=%fused_computation.20 | convolution fusion | flops 4646060032 | bytes 10684416 | tf_op jit(solution)/shard_map/dot_general | solution.py:285
  323.4 0.8 slice_add_fusion.8
  324.3 0.8 slice_add_fusion.7
  325.1 0.8 slice_add_fusion.6
  326.0 0.7 slice_add_fusion.11
  326.6 0.6 slice_add_fusion.14
  327.3 0.6 slice_add_fusion.17
  327.9 0.5 fusion.13
  329.2 1.8 fusion.6
  331.1 0.8 constant_dynamic-slice_fusion.3
  331.9 0.5 collective-permute-start
  333.1 2.0 dynamic-slice_add_fusion
  335.1 1.3 collective-permute-start.4
  336.4 1.9 dynamic-slice_add_fusion.1
  338.3 1.2 copy.8
  339.6 1.9 add_bitcast_fusion
  341.5 1.2 copy.9
  342.7 2.0 collective-permute-done
  344.7 1.1 add_bitcast_fusion.1
  345.9 4.6 %collective-permute-done.4 = f32[256,512]{1,0:T(8,128)} collective-permute-done((f32[256,512]{1,0:T(8,128)}, f32[256,512]{1,0:T(8,128)}, u32[]{:S(2)}, u32[]{:S(2)}) %collective-permute-start.4) | collective-permute-done | bytes 524320 | tf_op jit(solution)/shard_map/ppermute | solution.py:277
  350.5 1.1 fusion.7
  351.9 1.5 collective-permute-start.5
  353.4 2.2 collective-permute-done.5
  355.6 4.5 %collective-permute-done.7 = f32[512]{0:T(512)S(1)} collective-permute-done((f32[512]{0:T(512)S(1)}, f32[512]{0:T(512)S(1)}, u32[]{:S(2)}, u32[]{:S(2)}) %collective-permute-start.7) | collective-permute-done | bytes 2080 | tf_op jit(solution)/shard_map/ppermute | solution.py:21
  360.0 0.9 collective-permute-done.6
  361.5 1.6 copy.10
  (32 shorter events, 2.9 us)
Async XLA Ops:
  256.7 3.5 copy-start.2
  256.7 4.7 %copy-start.9 = (bf16[240,4096]{1,0:T(8,128)(2,1)S(1)}, bf16[240,4096]{1,0:T(8,128)(2,1)}, u32[]{:S(2)}) copy-start(bf16[240,4096]{1,0:T(8,128)(2,1)} %get-tuple-element.9) | copy-start | bytes 5898244
  256.7 6.2 %copy-start.10 = (bf16[240,4096]{1,0:T(8,128)(2,1)S(1)}, bf16[240,4096]{1,0:T(8,128)(2,1)}, u32[]{:S(2)}) copy-start(bf16[240,4096]{1,0:T(8,128)(2,1)} %get-tuple-element.12) | copy-start | bytes 5898244
  259.5 7.4 %copy-start.3 = (bf16[512,4096]{1,0:T(8,128)(2,1)}, bf16[512,4096]{1,0:T(8,128)(2,1)S(1)}, u32[]{:S(2)}) copy-start(bf16[512,4096]{1,0:T(8,128)(2,1)S(1)} %broadcast_select_fusion) | copy-start | bytes 12582916
  262.8 2.8 copy-start
  264.8 2.1 copy-start.5
  264.8 5.3 %copy-start.6 = (bf16[240,4096]{1,0:T(8,128)(2,1)}, bf16[240,4096]{1,0:T(8,128)(2,1)S(1)}, u32[]{:S(2)}) copy-start(bf16[240,4096]{1,0:T(8,128)(2,1)S(1)} %get-tuple-element.24) | copy-start | bytes 5898244
  284.7 8.2 %copy-start.1 = (bf16[512,4096]{1,0:T(8,128)(2,1)S(1)}, bf16[512,4096]{1,0:T(8,128)(2,1)}, u32[]{:S(2)}) copy-start(bf16[512,4096]{1,0:T(8,128)(2,1)} %broadcast_multiply_fusion.own) | copy-start | bytes 12582916
  284.7 8.2 %copy-start.4 = (bf16[512,4096]{1,0:T(8,128)(2,1)S(1)}, bf16[512,4096]{1,0:T(8,128)(2,1)}, u32[]{:S(2)}) copy-start(bf16[512,4096]{1,0:T(8,128)(2,1)} %copy-done.3) | copy-start | bytes 12582916
  290.0 43.1 %collective-permute-start.3 = (f32[256,512]{1,0:T(8,128)}, f32[256,512]{1,0:T(8,128)}, u32[]{:S(2)}, u32[]{:S(2)}) collective-permute-start(f32[256,512]{1,0:T(8,128)} %constant_dynamic-slice_fusion), channel_id=1, source_target_pairs={{0,1},{1,0},{2,3},{3,2},{4,5},{5,4},{6,7},{7,6},{8,9},{9,8},{10,11... | collective-permute-start | bytes 1572872 | tf_op jit(solution)/shard_map/ppermute | solution.py:277
  292.4 44.0 %collective-permute-start.2 = (f32[512,256]{1,0:T(8,128)}, f32[512,256]{1,0:T(8,128)}, u32[]{:S(2)}, u32[]{:S(2)}) collective-permute-start(f32[512,256]{1,0:T(8,128)} %constant_dynamic-slice_fusion.1), channel_id=1, source_target_pairs={{0,1},{1,0},{2,3},{3,2},{4,5},{5,4},{6,7},{7,6},{8,9},{9,8},{10,11... | collective-permute-start | bytes 1572872 | tf_op jit(solution)/shard_map/ppermute | solution.py:277
  308.1 1.1 copy-start.7
  309.2 30.3 %collective-permute-start.1 = (f32[512,256]{1,0:T(8,128)}, f32[512,256]{1,0:T(8,128)}, u32[]{:S(2)}, u32[]{:S(2)}) collective-permute-start(f32[512,256]{1,0:T(8,128)} %constant_dynamic-slice_fusion.2), channel_id=1, source_target_pairs={{0,1},{1,0},{2,3},{3,2},{4,5},{5,4},{6,7},{7,6},{8,9},{9,8},{10,11... | collective-permute-start | bytes 1572872 | tf_op jit(solution)/shard_map/ppermute | solution.py:277
  331.9 7.6 %copy-start.8 = (f32[512,512]{1,0:T(8,128)S(1)}, f32[512,512]{1,0:T(8,128)}, u32[]{:S(2)}) copy-start(f32[512,512]{1,0:T(8,128)} %copy-done.7) | copy-start | bytes 3145732
  331.9 12.8 %collective-permute-start = (f32[512,256]{0,1:T(8,128)}, f32[512,256]{0,1:T(8,128)}, u32[]{:S(2)}, u32[]{:S(2)}) collective-permute-start(f32[512,256]{0,1:T(8,128)} %constant_dynamic-slice_fusion.3), channel_id=1, source_target_pairs={{0,1},{1,0},{2,3},{3,2},{4,5},{5,4},{6,7},{7,6},{8,9},{9,8},{10,11... | collective-permute-start | bytes 1572872 | tf_op jit(solution)/shard_map/ppermute | solution.py:277
  335.1 15.4 %collective-permute-start.4 = (f32[256,512]{1,0:T(8,128)}, f32[256,512]{1,0:T(8,128)}, u32[]{:S(2)}, u32[]{:S(2)}) collective-permute-start(f32[256,512]{1,0:T(8,128)} %dynamic-slice_add_fusion), channel_id=1, source_target_pairs={{2,6},{4,0},{3,7},{5,1},{10,14},{12,8},{11,15},{13,9},{18,22},{20,... | collective-permute-start | bytes 1572872 | tf_op jit(solution)/shard_map/ppermute | solution.py:277
  351.9 3.6 %collective-permute-start.5 = (f32[512]{0:T(512)S(1)}, f32[512]{0:T(512)S(1)}, u32[]{:S(2)}, u32[]{:S(2)}) collective-permute-start(f32[512]{0:T(512)S(1)} %fusion.12), channel_id=1, source_target_pairs={{0,1},{1,0},{2,3},{3,2},{4,5},{5,4},{6,7},{7,6},{8,9},{9,8},{10,11... | collective-permute-start | bytes 6152 | tf_op jit(solution)/shard_map/ppermute | solution.py:277
  355.6 4.5 %collective-permute-start.7 = (f32[512]{0:T(512)S(1)}, f32[512]{0:T(512)S(1)}, u32[]{:S(2)}, u32[]{:S(2)}) collective-permute-start(f32[512]{0:T(512)S(1)} %add.196), channel_id=1, source_target_pairs={{4,0},{6,2},{0,4},{2,6},{5,1},{7,3},{1,5},{3,7},{12,8},{14,10},{8,... | collective-permute-start | bytes 6152 | tf_op jit(solution)/shard_map/ppermute | solution.py:21
  355.6 5.4 %collective-permute-start.6 = (f32[512]{0:T(512)S(1)}, f32[512]{0:T(512)S(1)}, u32[]{:S(2)}, u32[]{:S(2)}) collective-permute-start(f32[512]{0:T(512)S(1)} %add.196), channel_id=1, source_target_pairs={{6,0},{0,2},{2,4},{4,6},{7,1},{1,3},{3,5},{5,7},{14,8},{8,10},{10,... | collective-permute-start | bytes 6152 | tf_op jit(solution)/shard_map/ppermute | solution.py:21
